TPU v7x, 256 devices: a whole 4x4x8 slice. The times are simulated.
256 devices in a mesh: tm: 4 (over y), tile: 64 (over z, x, core).
Axes of the slice: x: 4, y: 4, z: 8, core: 2. Of those that a mesh axis runs over, the one named last changes fastest.
Arguments:
- frames: bfloat16 [4, 64, 96, 7680], P('tm', 'tile'), may hold values from -6 to 6
- first_gain: float32 [96], replicated, may hold values from 0.4 to 1.6
- first_weight: bfloat16 [27, 9216], replicated, may hold values from -0.125 to 0.125
- first_bias: float32 [96], replicated, may hold values from -3 to 3
- second_gain: float32 [96], replicated, may hold values from 0.4 to 1.6
- second_weight: bfloat16 [27, 9216], replicated, may hold values from -0.125 to 0.125
- second_bias: float32 [96], replicated, may hold values from -3 to 3
Outputs:
- encoded: bfloat16 [4, 64, 96, 7680], P('tm', 'tile')
All inputs are finite; a program needn't handle non-finite values.
Results may differ from a plain program's by a relative error of at most 0.0032.
Values may be sent and summed in bfloat16 or wider, within the bound.
No kernel may reach another device: no remote copies, remote signals or barrier semaphores. Data moves between devices by JAX's collectives and lax.ppermute only.
A program may use at most 128 MiB of HBM per device.

v0:
```python
import functools

import jax
import jax.numpy as jnp
import numpy as np
from jax import lax
from jax.experimental import pallas as pl
from jax.experimental.pallas import tpu as pltpu
from jax.sharding import PartitionSpec as P

C = 96
TROWS = 8
TCOLS = 8
HT = 48
WT = 160
FRAMES = 4
STRIP = HT // FRAMES
LANES = STRIP * WT
PARTS = ((0, 8), (8, 4))

PITCH = WT + 4
EXT = 2688
PLACED = 2176
INSET = 2 * PITCH + 2
QUADS = 4 * (STRIP + 4)
RIM = 768
SIDES = 256
TILE = 256

eps = 1e-06
MIB = 1024 * 1024


def call(kernel, outs, scratch, args, out_space=pltpu.VMEM, mib=8, flops=0, moved=0, **more):
    specs = [pl.BlockSpec(memory_space=space) for space, _ in args]
    arrays = [array for _, array in args]
    if not isinstance(out_space, tuple):
        out_space = (out_space,) * len(outs)
    return pl.pallas_call(
        kernel,
        out_shape=[jax.ShapeDtypeStruct(s, jnp.bfloat16) for s in outs],
        in_specs=specs,
        out_specs=[pl.BlockSpec(memory_space=space) for space in out_space],
        scratch_shapes=scratch,
        compiler_params=pltpu.CompilerParams(vmem_limit_bytes=mib * MIB),
        cost_estimate=pl.CostEstimate(flops=flops, bytes_accessed=moved, transcendentals=0),
        **more,
    )(*arrays)


def smem(*arrays):
    return [(pltpu.SMEM, a) for a in arrays]


def vmem(*arrays):
    return [(pltpu.VMEM, a) for a in arrays]


def anywhere(*arrays):
    return [(pl.ANY, a) for a in arrays]


def activated(values, gain):
    mean_square = jnp.sum(values * values, axis=0, keepdims=True) * (1.0 / C)
    scaled = values * lax.rsqrt(mean_square + eps) * gain
    half = 0.5 * scaled
    return half * jnp.tanh(half) + half


def upright(row):
    at = lax.broadcasted_iota(jnp.int32, (C, C), 0) == lax.broadcasted_iota(jnp.int32, (C, C), 1)
    return jnp.sum(jnp.where(at, row, 0.0), axis=1, keepdims=True)


def strip_at(k, me):
    return pl.multiple_of(lax.rem(me + k, FRAMES) * LANES, 128)


def frame_of(k, me):
    return lax.rem(me - k + FRAMES, FRAMES)


def run_all(copies):
    for copy in copies:
        copy.start()
    for copy in copies:
        copy.wait()


def cut_kernel(me_ref, x, m1, m2, m3, sems):
    run_all(
        [
            pltpu.make_async_copy(
                x.at[:, pl.ds(strip_at(k + 1, me_ref[0]), LANES)], out, sems.at[k]
            )
            for k, out in enumerate((m1, m2, m3))
        ]
    )


def edge_kernel(x, top, bottom, quads):
    top[...] = x[:, : 2 * WT]
    bottom[...] = x[:, (HT - 2) * WT :]
    quads[...] = jnp.zeros_like(quads)
    for i in range(HT):
        at = 4 * (i + 2)
        quads[:, at : at + 2] = x[:, (i + 1) * WT - 2 : (i + 1) * WT]
        quads[:, at + 2 : at + 4] = x[:, i * WT : i * WT + 2]


def side_kernel(me_ref, exists, x, above, below, quads, out, rows_out):
    me = me_ref[0]
    out[...] = quads[...]
    for rows, row, there in ((above, 0, exists[0]), (below, HT + 2, exists[1])):
        for i in range(2):
            at = 4 * (row + i)
            first = rows[:, i * WT : i * WT + 2]
            last = rows[:, (i + 1) * WT - 2 : (i + 1) * WT]
            out[:, at : at + 2] = jnp.where(there > 0, last, jnp.zeros_like(last))
            out[:, at + 2 : at + 4] = jnp.where(there > 0, first, jnp.zeros_like(first))
    for q in range(FRAMES):
        k = lax.rem(q - me + FRAMES, FRAMES)
        start = q * LANES
        if q == 0:
            upper = jnp.where(exists[0] > 0, above[...], jnp.zeros_like(above))
        else:
            upper = x[:, start - 2 * WT : start]
        if q == FRAMES - 1:
            lower = jnp.where(exists[1] > 0, below[...], jnp.zeros_like(below))
        else:
            lower = x[:, start + LANES : start + LANES + 2 * WT]
        rows_out[k, :, : 2 * WT] = upper
        rows_out[k, :, 2 * WT :] = lower


def rim_kernel(me_ref, exists, rows, from_left, from_right, *outs):
    me = me_ref[0]
    lane = lax.broadcasted_iota(jnp.int32, (C, SIDES), 1) % 4
    left = jnp.where(exists[2] > 0, from_left[...], jnp.zeros_like(from_left))
    right = jnp.where(exists[3] > 0, from_right[...], jnp.zeros_like(from_right))
    others = jnp.where(lane < 2, left.astype(jnp.float32), right.astype(jnp.float32))
    for k in range(FRAMES):
        strip = lax.rem(me + k, FRAMES)
        outs[k][:, : 4 * WT] = rows[k]
        mine = pltpu.roll(others, lax.rem(SIDES - 4 * STRIP * strip, SIDES), 1)
        outs[k][:, 4 * WT :] = mine[:, :128].astype(jnp.bfloat16)


def early_kernel(me_ref, gain, x, m1, m2, m3, acts, placed, held, sems):
    me = me_ref[0]
    own = x.at[:, pl.ds(strip_at(0, me), LANES)]
    copies = [
        pltpu.make_async_copy(ref, held.at[frame_of(k, me)], sems.at[k])
        for k, ref in enumerate((own, m1, m2, m3))
    ]
    run_all(copies)
    gain = upright(gain[...])
    wide = STRIP * PITCH
    for t in range(FRAMES):
        for i in range(STRIP):
            placed[t, :, i * PITCH : i * PITCH + WT] = held[t, :, i * WT : (i + 1) * WT]
        act = activated(placed[t, :, :2048].astype(jnp.float32), gain).astype(jnp.bfloat16)
        acts[t, :, INSET : INSET + wide] = act[:, :wide]


def up128(n):
    return (n + 127) // 128 * 128


class Sizes:
    def __init__(self, first, rows):
        self.hidden = up128((rows + 2) * PITCH)
        self.out = up128(rows * PITCH)
        self.ext_at = first * PITCH // 128 * 128
        self.ext = up128((first + 2) * PITCH + self.hidden) - self.ext_at
        self.placed = up128(first * PITCH + self.out) - self.ext_at
        self.held = max(self.hidden, up128(2 * PITCH + self.out))


def together(tiles, tasks):
    for n, tile in enumerate(tiles):
        tile()
        for task in tasks[n * len(tasks) // len(tiles) : (n + 1) * len(tasks) // len(tiles)]:
            task()


def block_kernel(first, rows, me_ref, exists, *refs):
    acts, placed_in, r0, r1, r2, r3, w1, w2 = refs[:8]
    outs = refs[12:16]
    ext, placed, rims, rim_acts, lifted, lifted2, parts, parts2, held, total, results, sems = refs[16:]
    size = Sizes(first, rows)
    me = me_ref[0]
    copies = [
        pltpu.make_async_copy(acts.at[:, :, pl.ds(size.ext_at, size.ext)], ext, sems.at[0]),
        pltpu.make_async_copy(
            placed_in.at[:, :, pl.ds(size.ext_at, size.placed)], placed, sems.at[1]
        ),
    ]
    for k, rim in enumerate((r0, r1, r2, r3)):
        copies.append(pltpu.make_async_copy(rim, rims.at[frame_of(k, me)], sems.at[2 + k]))
    for copy in copies:
        copy.start()
    g1, b1, g2, b2 = (upright(ref[...]) for ref in refs[8:12])
    mask = inside(first, rows, me, exists)
    for copy in copies:
        copy.wait()

    def spans(lanes):
        return [(at, min(TILE, lanes - at)) for at in range(0, lanes, TILE)]

    def lift(t):
        def rim_step():
            rim_acts[t] = activated(rims[t].astype(jnp.float32), g1).astype(jnp.bfloat16)

        def row_step(i):
            at = i * PITCH + 2 - size.ext_at
            if i < 2:
                ext[t, :, at : at + WT] = rim_acts[t, :, i * WT : (i + 1) * WT]
            if i >= STRIP + 2:
                near = (i - STRIP) * WT
                ext[t, :, at : at + WT] = rim_acts[t, :, near : near + WT]
            side = 4 * WT + 4 * i
            if i == first:
                ext[t, :, at - 2 : at] = rim_acts[t, :, side : side + 2]
            last = 2 if i == first + rows + 3 else 4
            ext[t, :, at + WT : at + WT + last] = rim_acts[t, :, side + 2 : side + 2 + last]

        def copy_step(di, at, wide):
            start = (first + di) * PITCH - size.ext_at + at
            lifted[t, di * C : (di + 1) * C, at : at + wide] = ext[t, :, start : start + wide]

        steps = [rim_step]
        steps += [functools.partial(row_step, i) for i in range(first, first + rows + 4)]
        for at, wide in spans(size.hidden):
            steps += [functools.partial(copy_step, di, at, wide) for di in range(3)]
        return steps

    def products(t, w, operand, to, lanes):
        frames = min(t + 1, 3)
        depth = frames * 3 * C

        def step(at, wide):
            tile = operand[t + 1 - frames : t + 1, :, at : at + wide].reshape(depth, wide)
            to[t % 2, :, at : at + wide] = jnp.dot(
                w[:, 9 * C - depth :], tile, preferred_element_type=jnp.float32
            )

        return [functools.partial(step, at, wide) for at, wide in spans(lanes)]

    def gathered(source, t, at, wide, lanes):
        reach = min(wide + 128, lanes - at)
        field = source[t % 2, 0:C, at : at + wide]
        for dj in (1, 2):
            part = source[t % 2, dj * C : (dj + 1) * C, at : at + reach]
            field = field + pltpu.roll(part, reach - dj, 1)[:, :wide]
        return field

    def middle(t):
        def step(at, wide):
            values = gathered(parts, t, at, wide, size.hidden) + b1
            values = activated(values, g2) * mask[:, at : at + wide]
            held[t % 2, :, at : at + wide] = values.astype(jnp.bfloat16)

        return [functools.partial(step, at, wide) for at, wide in spans(size.hidden)]

    def lift2(t):
        def step(di, at, wide):
            start = di * PITCH + at
            to = lifted2.at[t, pl.ds(di * C, C), pl.ds(at, wide)]
            to[...] = held[t % 2, :, start : start + wide]

        return [
            functools.partial(step, di, at, wide) for at, wide in spans(size.out) for di in range(3)
        ]

    def finish(t):
        def step(at, wide):
            start = first * PITCH - size.ext_at + at
            values = gathered(parts2, t, at, wide, size.out) + b2
            values = values + placed[t, :, start : start + wide].astype(jnp.float32)
            total[t % 2, :, at : at + wide] = values.astype(jnp.bfloat16)

        return [functools.partial(step, at, min(wide, size.placed - at)) for at, wide in spans(size.out)]

    def compact(t):
        def step(i):
            row = total[t % 2, :, i * PITCH : i * PITCH + WT]
            results[t, :, i * WT : (i + 1) * WT] = row

        return [functools.partial(step, i) for i in range(rows)]

    def first_products(t):
        return products(t, w1, lifted, parts, size.hidden)

    def second_products(t):
        return products(t, w2, lifted2, parts2, size.out)

    for step in lift(0):
        step()
    together(first_products(0), lift(1))
    together(first_products(1), middle(0) + lift(2))
    together(first_products(2), lift2(0) + middle(1) + lift(3))
    together(second_products(0), lift2(1) + middle(2))
    together(first_products(3), lift2(2) + finish(0))
    together(second_products(1), middle(3) + compact(0))
    together(second_products(2), lift2(3) + finish(1) + compact(1))
    together(second_products(3), finish(2) + compact(2))
    for step in finish(3) + compact(3):
        step()
    run_all(
        [
            pltpu.make_async_copy(results.at[frame_of(k, me)], outs[k], sems.at[k])
            for k in range(FRAMES)
        ]
    )


def place_kernel(me_ref, *refs):
    pieces, out, sems = refs[:-2], refs[-2], refs[-1]
    copies = []
    for part, (first, rows) in enumerate(PARTS):
        for k in range(FRAMES):
            start = pl.multiple_of(strip_at(k, me_ref[0]) + first * WT, 128)
            place = out.at[:, pl.ds(start, rows * WT)]
            n = part * FRAMES + k
            copies.append(pltpu.make_async_copy(pieces[n], place, sems.at[n]))
    run_all(copies)


def weight_kernel(first, second, first_out, second_out):
    for ref, out in ((first, first_out), (second, second_out)):
        for dj in range(3):
            for n in range(9):
                out[dj * C : (dj + 1) * C, n * C : (n + 1) * C] = ref[n * 3 + dj]


def over_time(array, by):
    pairs = [(i, (i + by) % FRAMES) for i in range(FRAMES)]
    return lax.ppermute(array, "tm", pairs)


def over_tiles(array, down, right):
    pairs = [
        (i * TCOLS + j, (i + down) % TROWS * TCOLS + (j + right) % TCOLS)
        for i in range(TROWS)
        for j in range(TCOLS)
    ]
    return lax.ppermute(array, "tile", pairs)


def inside(first, rows, me, exists):
    lane = lax.broadcasted_iota(jnp.int32, (1, Sizes(first, rows).hidden), 1)
    outside = jnp.zeros(lane.shape, jnp.int32)
    if first == 0:
        absent = jnp.where(jnp.logical_or(me > 0, exists[0] > 0), 0, 1)
        outside += jnp.where(lane < PITCH, absent, 0)
    if first + rows == STRIP:
        absent = jnp.where(jnp.logical_or(me < FRAMES - 1, exists[1] > 0), 0, 1)
        outside += jnp.where(lane >= (rows + 1) * PITCH, absent, 0)
    for i in range(rows + 2):
        outside += jnp.where(lane == i * PITCH, 1 - exists[2], 0)
        outside += jnp.where(lane == i * PITCH + WT + 1, 1 - exists[3], 0)
    return jnp.where(outside > 0, 0.0, 1.0)


def block(first, rows, me, exists, sources, common):
    size = Sizes(first, rows)
    scratch = [
        pltpu.VMEM((FRAMES, C, size.ext), jnp.bfloat16),
        pltpu.VMEM((FRAMES, C, size.placed), jnp.bfloat16),
        pltpu.VMEM((FRAMES, C, RIM), jnp.bfloat16),
        pltpu.VMEM((FRAMES, C, RIM), jnp.bfloat16),
        pltpu.VMEM((FRAMES, 3 * C, size.hidden), jnp.bfloat16),
        pltpu.VMEM((FRAMES, 3 * C, size.out), jnp.bfloat16),
        pltpu.VMEM((2, 3 * C, size.hidden), jnp.float32),
        pltpu.VMEM((2, 3 * C, size.out), jnp.float32),
        pltpu.VMEM((2, C, size.held), jnp.bfloat16),
        pltpu.VMEM((2, C, size.out), jnp.bfloat16),
        pltpu.VMEM((FRAMES, C, rows * WT), jnp.bfloat16),
        pltpu.SemaphoreType.DMA((6,)),
    ]
    return call(
        functools.partial(block_kernel, first, rows),
        [(C, rows * WT)] * FRAMES,
        scratch,
        smem(me, exists) + anywhere(*sources) + vmem(*common),
        out_space=pl.ANY,
        flops=2 * 27 * C * C * (2 * rows + 2) * WT * 3,
        mib=28,
        moved=8 * MIB,
        name="block_%d" % first,
    )


def on_device(
    frames, first_gain, first_weight, first_bias, second_gain, second_weight, second_bias
):
    x = frames.reshape(C, HT * WT)
    at_time = lax.axis_index("tm")
    tile = lax.axis_index("tile")
    me = at_time.astype(jnp.int32).reshape(1)
    tile_row, tile_column = tile // TCOLS, tile % TCOLS
    exists = jnp.stack(
        [tile_row > 0, tile_row < TROWS - 1, tile_column > 0, tile_column < TCOLS - 1]
    ).astype(jnp.int32)
    dma = pltpu.SemaphoreType.DMA

    mains = call(
        cut_kernel,
        [(C, LANES)] * 3,
        [dma((3,))],
        smem(me) + anywhere(x),
        out_space=pl.ANY,
        moved=6 * C * LANES,
        name="cut",
    )
    mains = [over_time(main, k + 1) for k, main in enumerate(mains)]
    top, bottom, quads = call(
        edge_kernel,
        [(C, 2 * WT)] * 2 + [(C, SIDES)],
        [],
        vmem(x),
        moved=2 * C * HT * WT,
        name="edges",
    )
    above = over_tiles(bottom, 1, 0)
    below = over_tiles(top, -1, 0)
    quads, rows = call(
        side_kernel,
        [(C, SIDES), (FRAMES, C, 4 * WT)],
        [],
        smem(me, exists) + vmem(x, above, below, quads),
        moved=8 * C * SIDES,
        name="sides",
    )
    from_left = over_tiles(quads, 0, 1)
    from_right = over_tiles(quads, 0, -1)
    rims = call(
        rim_kernel,
        [(C, RIM)] * FRAMES,
        [],
        smem(me, exists) + vmem(rows, from_left, from_right),
        moved=8 * C * RIM,
        name="rims",
    )
    own_rim, me_late, first_weight, second_weight = lax.optimization_barrier(
        (rims[0], me, first_weight, second_weight)
    )
    rims = [own_rim] + [over_time(rims[k], k) for k in (1, 2, 3)]
    w1, w2 = call(
        weight_kernel,
        [(3 * C, 9 * C)] * 2,
        [],
        vmem(first_weight.reshape(27, C, C), second_weight.reshape(27, C, C)),
        moved=8 * 27 * C * C,
        name="weights",
    )
    acts, placed = call(
        early_kernel,
        [(FRAMES, C, EXT), (FRAMES, C, PLACED)],
        [pltpu.VMEM((FRAMES, C, LANES), jnp.bfloat16), dma((FRAMES,))],
        smem(me_late) + vmem(first_gain[None]) + anywhere(x, *mains),
        mib=12,
        moved=8 * MIB,
        name="early",
    )
    pieces = []
    scales = [a[None] for a in (first_gain, first_bias, second_gain, second_bias)]
    for first, rows in PARTS:
        me_block = me if not pieces else pieces[-1][1]
        outs = block(first, rows, me_block, exists, [acts, placed, *rims], [w1, w2, *scales])
        if pieces:
            outs, before = lax.optimization_barrier((outs, pieces[-1][0]))
            pieces[-1] = (before, None)
        own, me_block = lax.optimization_barrier((outs[0], me))
        pieces.append(([own] + [over_time(outs[k], -k) for k in (1, 2, 3)], me_block))
    pieces = [piece for part, _ in pieces for piece in part]
    (encoded,) = call(
        place_kernel,
        [(C, HT * WT)],
        [dma((len(pieces),))],
        smem(me) + anywhere(*pieces),
        out_space=pl.ANY,
        name="place",
    )
    return encoded.reshape(1, 1, C, HT * WT)


def solution(mesh):
    return jax.shard_map(
        on_device,
        mesh=mesh,
        in_specs=(P("tm", "tile", None, None), P(), P(), P(), P(), P(), P()),
        out_specs=P("tm", "tile", None, None),
        check_vma=False,
    )
```

profile of v0, /device:TPU:98, one launch (start us, length us, event | category | flops | bytes accessed | tf_op | source)
XLA Modules:
  0.0 77.2 jit_solution(4441741190463572378)
XLA Ops:
  0.0 0.0 copy-start
  0.0 1.4 %copy-done = bf16[1,1,96,7680]{3,2,1,0:T(8,128)(2,1)S(1)} copy-done((bf16[1,1,96,7680]{3,2,1,0:T(8,128)(2,1)S(1)}, bf16[1,1,96,7680]{3,2,1,0:T(8,128)(2,1)}, u32[]{:S(2)}) %copy-start) | copy-done | bytes 1474584
  1.4 0.0 copy-start.1
  1.4 0.9 %cut.1 = (bf16[96,1920]{1,0:T(8,128)(2,1)S(1)}, bf16[96,1920]{1,0:T(8,128)(2,1)}, bf16[96,1920]{1,0:T(8,128)(2,1)}) custom-call(s32[1]{0:T(128)} %bitcast.me_ref, bf16[96,7680]{1,0:T(8,128)(2,1)S(1)} %bitcast.11), custom_call_target="tpu_custom_call" | custom-call | bytes 1105920 | tf_op jit(solution)/shard_map/cut/pallas_call | solution.py:39
  2.3 1.7 %collective-permute-start.4 = (bf16[96,1920]{1,0:T(8,128)(2,1)S(1)}, bf16[96,1920]{1,0:T(8,128)(2,1)S(1)}, u32[]{:S(2)}, u32[]{:S(2)}) collective-permute-start(bf16[96,1920]{1,0:T(8,128)(2,1)S(1)} %get-tuple-element.51), channel_id=1, source_target_pairs={{0,64},{64,128},{128,192},{192,0},{1,65},{65,129},{129,193},{193,1... | collective-permute-start | bytes 1105928 | tf_op jit(solution)/shard_map/ppermute | solution.py:339
  4.0 2.9 %collective-permute-start.5 = (bf16[96,1920]{1,0:T(8,128)(2,1)}, bf16[96,1920]{1,0:T(8,128)(2,1)S(1)}, u32[]{:S(2)}, u32[]{:S(2)}) collective-permute-start(bf16[96,1920]{1,0:T(8,128)(2,1)} %get-tuple-element.52), channel_id=1, source_target_pairs={{0,128},{64,192},{128,0},{192,64},{1,129},{65,193},{129,1},{193,65... | collective-permute-start | bytes 1105928 | tf_op jit(solution)/shard_map/ppermute | solution.py:339
  6.9 0.0 copy-start.8
  6.9 1.3 %collective-permute-start.6 = (bf16[96,1920]{1,0:T(8,128)(2,1)}, bf16[96,1920]{1,0:T(8,128)(2,1)}, u32[]{:S(2)}, u32[]{:S(2)}) collective-permute-start(bf16[96,1920]{1,0:T(8,128)(2,1)} %get-tuple-element.53), channel_id=1, source_target_pairs={{0,192},{64,0},{128,64},{192,128},{1,193},{65,1},{129,65},{193,129... | collective-permute-start | bytes 1105928 | tf_op jit(solution)/shard_map/ppermute | solution.py:339
  8.2 0.0 copy-done.1
  8.2 1.3 %edges.1 = (bf16[96,320]{1,0:T(8,128)(2,1)S(1)}, bf16[96,320]{1,0:T(8,128)(2,1)S(1)}, bf16[96,256]{1,0:T(8,128)(2,1)S(1)}) custom-call(bf16[96,7680]{1,0:T(8,128)(2,1)S(1)} %bitcast.12), custom_call_target="tpu_custom_call" | custom-call | bytes 1474560 | tf_op jit(solution)/shard_map/edges/pallas_call | solution.py:39
  9.5 3.2 %collective-permute-start = (bf16[96,320]{1,0:T(8,128)(2,1)S(1)}, bf16[96,320]{1,0:T(8,128)(2,1)S(1)}, u32[]{:S(2)}, u32[]{:S(2)}) collective-permute-start(bf16[96,320]{1,0:T(8,128)(2,1)S(1)} %get-tuple-element.44), channel_id=1, source_target_pairs={{0,8},{1,9},{2,10},{3,11},{4,12},{5,13},{6,14},{7,15},{8,16},{9,17... | collective-permute-start | bytes 184328 | tf_op jit(solution)/shard_map/ppermute | solution.py:348
  12.7 0.0 collective-permute-start.1
  12.7 0.1 add_convert_fusion.exists
  12.8 1.9 %collective-permute-done.above = bf16[96,320]{1,0:T(8,128)(2,1)S(1)} collective-permute-done((bf16[96,320]{1,0:T(8,128)(2,1)S(1)}, bf16[96,320]{1,0:T(8,128)(2,1)S(1)}, u32[]{:S(2)}, u32[]{:S(2)}) %collective-permute-start) | collective-permute-done | bytes 61472 | tf_op jit(solution)/shard_map/ppermute | solution.py:348
  14.7 3.6 %collective-permute-done.1.below = bf16[96,320]{1,0:T(8,128)(2,1)S(1)} collective-permute-done((bf16[96,320]{1,0:T(8,128)(2,1)S(1)}, bf16[96,320]{1,0:T(8,128)(2,1)S(1)}, u32[]{:S(2)}, u32[]{:S(2)}) %collective-permute-start.1) | collective-permute-done | bytes 61472 | tf_op jit(solution)/shard_map/ppermute | solution.py:348
  18.3 0.9 %sides.1 = (bf16[96,256]{1,0:T(8,128)(2,1)S(1)}, bf16[4,96,640]{2,1,0:T(8,128)(2,1)S(1)}) custom-call(s32[1]{0:T(128)} %bitcast.me_ref, s32[4]{0:T(128)S(1)} %add_convert_fusion.exists, bf16[96,7680]{1,0:T(8,128)(2,1)S(1)} %bitcast.13, bf16[96,320]{1,0:T(8,128)(2,1)S(1)} %collective-permute-done.above, bf16[96,320]{1,0:T(8,128)(2,1)S(1)} %collective-permute-done.1.below, ...), custom_call_target="tpu_custom_call" | custom-call | bytes 196608 | tf_op jit(solution)/shard_map/sides/pallas_call | solution.py:39
  19.2 0.0 collective-permute-start.3
  19.2 0.5 collective-permute-start.2
  19.7 1.2 %collective-permute-done.3.from_right = bf16[96,256]{1,0:T(8,128)(2,1)S(1)} collective-permute-done((bf16[96,256]{1,0:T(8,128)(2,1)S(1)}, bf16[96,256]{1,0:T(8,128)(2,1)S(1)}, u32[]{:S(2)}, u32[]{:S(2)}) %collective-permute-start.3) | collective-permute-done | bytes 49184 | tf_op jit(solution)/shard_map/ppermute | solution.py:348
  21.0 1.8 %collective-permute-done.2.from_left = bf16[96,256]{1,0:T(8,128)(2,1)S(1)} collective-permute-done((bf16[96,256]{1,0:T(8,128)(2,1)S(1)}, bf16[96,256]{1,0:T(8,128)(2,1)S(1)}, u32[]{:S(2)}, u32[]{:S(2)}) %collective-permute-start.2) | collective-permute-done | bytes 49184 | tf_op jit(solution)/shard_map/ppermute | solution.py:348
  22.7 1.4 %rims.1 = (bf16[96,768]{1,0:T(8,128)(2,1)S(1)}, bf16[96,768]{1,0:T(8,128)(2,1)}, bf16[96,768]{1,0:T(8,128)(2,1)}, bf16[96,768]{1,0:T(8,128)(2,1)}) custom-call(s32[1]{0:T(128)} %bitcast.me_ref, s32[4]{0:T(128)S(1)} %add_convert_fusion.exists, bf16[4,96,640]{2,1,0:T(8,128)(2,1)S(1)} %get-tuple-element.47.rows, ...), custom_call_target="tpu_custom_call" | custom-call | bytes 589824 | tf_op jit(solution)/shard_map/rims/pallas_call | solution.py:39
  24.2 0.0 copy-start.3
  24.2 0.7 copy-done.3
  24.8 0.7 collective-permute-start.7
  25.5 0.8 %collective-permute-start.8 = (bf16[96,768]{1,0:T(8,128)(2,1)}, bf16[96,768]{1,0:T(8,128)(2,1)}, u32[]{:S(2)}, u32[]{:S(2)}) collective-permute-start(bf16[96,768]{1,0:T(8,128)(2,1)} %get-tuple-element.58), channel_id=1, source_target_pairs={{0,128},{64,192},{128,0},{192,64},{1,129},{65,193},{129,1},{193,65... | collective-permute-start | bytes 442376 | tf_op jit(solution)/shard_map/ppermute | solution.py:339
  26.3 0.0 collective-permute-done.4.m1
  26.3 1.9 %collective-permute-start.9 = (bf16[96,768]{1,0:T(8,128)(2,1)}, bf16[96,768]{1,0:T(8,128)(2,1)}, u32[]{:S(2)}, u32[]{:S(2)}) collective-permute-start(bf16[96,768]{1,0:T(8,128)(2,1)} %get-tuple-element.59), channel_id=1, source_target_pairs={{0,192},{64,0},{128,64},{192,128},{1,193},{65,1},{129,65},{193,129... | collective-permute-start | bytes 442376 | tf_op jit(solution)/shard_map/ppermute | solution.py:339
  28.2 0.0 copy-done.8
  28.2 0.0 copy-start.2
  28.2 0.7 reshape.17.first
  28.8 1.7 %reshape.18.second = bf16[27,96,96]{2,1,0:T(8,128)(2,1)S(1)} reshape(bf16[27,9216]{1,0:T(8,128)(2,1)} %param.12) | data formatting | bytes 995328 | tf_op jit(solution)/shard_map/reshape | solution.py:454
  30.6 0.0 copy-start.4
  30.6 0.0 copy-start.5
  30.6 0.0 copy-start.6
  30.6 0.0 copy-start.7
  30.6 0.5 weights.1
  31.1 0.0 collective-permute-done.5.m2
  31.1 0.0 collective-permute-done.6.m3
  31.2 0.0 copy-done.2
  31.2 3.6 %early.1 = (bf16[4,96,2688]{2,1,0:T(8,128)(2,1)S(1)}, bf16[4,96,2176]{2,1,0:T(8,128)(2,1)S(1)}) custom-call(s32[1]{0:T(128)} %bitcast.me_ref, f32[1,96]{1,0:T(1,128)S(1)} %bitcast.15, bf16[96,7680]{1,0:T(8,128)(2,1)S(1)} %bitcast.14, bf16[96,1920]{1,0:T(8,128)(2,1)S(1)} %collective-permute-done.4.m1, bf16[96,1920]{1,0:T(8,128)(2,1)S(1)} %collective-permute-done.5.m2, ...), custom_call_target="tpu_custom_call" | custom-call | bytes 8388608 | tf_op jit(solution)/shard_map/early/pallas_call | solution.py:39
  34.7 0.8 collective-permute-done.7.refs_3_
  35.5 0.0 collective-permute-done.8.refs_4_
  35.5 0.6 collective-permute-done.9.refs_5_
  36.1 0.0 copy-done.4
  36.1 0.0 copy-done.5
  36.1 0.0 copy-done.6
  36.1 0.0 copy-done.7
  36.2 14.2 %block_0.1 = (bf16[96,1280]{1,0:T(8,128)(2,1)S(1)}, bf16[96,1280]{1,0:T(8,128)(2,1)S(1)}, bf16[96,1280]{1,0:T(8,128)(2,1)S(1)}, bf16[96,1280]{1,0:T(8,128)(2,1)S(1)}) custom-call(s32[1]{0:T(128)} %bitcast.me_ref, s32[4]{0:T(128)S(1)} %add_convert_fusion.exists, bf16[4,96,2688]{2,1,0:T(8,128)(2,1)S(1)} %get-tuple-element.54.refs_0_, ...), custom_call_target="tpu_custom_call" | custom-call | flops 4299816960 | bytes 8388608 | tf_op jit(solution)/shard_map/block_0/pallas_call | solution.py:39
  50.4 2.5 %collective-permute-start.10 = (bf16[96,1280]{1,0:T(8,128)(2,1)S(1)}, bf16[96,1280]{1,0:T(8,128)(2,1)S(1)}, u32[]{:S(2)}, u32[]{:S(2)}) collective-permute-start(bf16[96,1280]{1,0:T(8,128)(2,1)S(1)} %get-tuple-element.71), channel_id=1, source_target_pairs={{0,192},{64,0},{128,64},{192,128},{1,193},{65,1},{129,65},{193,129... | collective-permute-start | bytes 737288 | tf_op jit(solution)/shard_map/ppermute | solution.py:339
  52.9 0.0 collective-permute-start.11
  52.9 1.0 %collective-permute-start.12 = (bf16[96,1280]{1,0:T(8,128)(2,1)S(1)}, bf16[96,1280]{1,0:T(8,128)(2,1)S(1)}, u32[]{:S(2)}, u32[]{:S(2)}) collective-permute-start(bf16[96,1280]{1,0:T(8,128)(2,1)S(1)} %get-tuple-element.73), channel_id=1, source_target_pairs={{0,64},{64,128},{128,192},{192,0},{1,65},{65,129},{129,193},{193,1... | collective-permute-start | bytes 737288 | tf_op jit(solution)/shard_map/ppermute | solution.py:339
  53.9 9.5 %block_8.1 = (bf16[96,640]{1,0:T(8,128)(2,1)S(1)}, bf16[96,640]{1,0:T(8,128)(2,1)S(1)}, bf16[96,640]{1,0:T(8,128)(2,1)S(1)}, bf16[96,640]{1,0:T(8,128)(2,1)S(1)}) custom-call(s32[1]{0:T(128)} %bitcast.me_ref, s32[4]{0:T(128)S(1)} %add_convert_fusion.exists, bf16[4,96,2688]{2,1,0:T(8,128)(2,1)S(1)} %get-tuple-element.54.refs_0_, ...), custom_call_target="tpu_custom_call" | custom-call | flops 2388787200 | bytes 8388608 | tf_op jit(solution)/shard_map/block_8/pallas_call | solution.py:39
  63.4 0.0 collective-permute-done.10.refs_1_
  63.4 0.0 collective-permute-done.11.refs_2_
  63.4 3.4 %collective-permute-done.12.refs_3_ = bf16[96,1280]{1,0:T(8,128)(2,1)S(1)} collective-permute-done((bf16[96,1280]{1,0:T(8,128)(2,1)S(1)}, bf16[96,1280]{1,0:T(8,128)(2,1)S(1)}, u32[]{:S(2)}, u32[]{:S(2)}) %collective-permute-start.12) | collective-permute-done | bytes 245792 | tf_op jit(solution)/shard_map/ppermute | solution.py:339
  66.8 0.9 %collective-permute-start.13 = (bf16[96,640]{1,0:T(8,128)(2,1)S(1)}, bf16[96,640]{1,0:T(8,128)(2,1)S(1)}, u32[]{:S(2)}, u32[]{:S(2)}) collective-permute-start(bf16[96,640]{1,0:T(8,128)(2,1)S(1)} %get-tuple-element.80), channel_id=1, source_target_pairs={{0,192},{64,0},{128,64},{192,128},{1,193},{65,1},{129,65},{193,129... | collective-permute-start | bytes 368648 | tf_op jit(solution)/shard_map/ppermute | solution.py:339
  67.7 0.4 collective-permute-start.14
  68.1 0.8 collective-permute-start.15
  68.9 4.2 %collective-permute-done.13.refs_5_ = bf16[96,640]{1,0:T(8,128)(2,1)S(1)} collective-permute-done((bf16[96,640]{1,0:T(8,128)(2,1)S(1)}, bf16[96,640]{1,0:T(8,128)(2,1)S(1)}, u32[]{:S(2)}, u32[]{:S(2)}) %collective-permute-start.13) | collective-permute-done | bytes 122912 | tf_op jit(solution)/shard_map/ppermute | solution.py:339
  73.0 2.3 %collective-permute-done.14.refs_6_ = bf16[96,640]{1,0:T(8,128)(2,1)S(1)} collective-permute-done((bf16[96,640]{1,0:T(8,128)(2,1)S(1)}, bf16[96,640]{1,0:T(8,128)(2,1)S(1)}, u32[]{:S(2)}, u32[]{:S(2)}) %collective-permute-start.14) | collective-permute-done | bytes 122912 | tf_op jit(solution)/shard_map/ppermute | solution.py:339
  75.3 0.5 collective-permute-done.15.refs_7_
  75.9 1.2 %place.1 = bf16[96,7680]{1,0:T(8,128)(2,1)} custom-call(s32[1]{0:T(128)} %bitcast.me_ref, bf16[96,1280]{1,0:T(8,128)(2,1)S(1)} %get-tuple-element.74.refs_0_, bf16[96,1280]{1,0:T(8,128)(2,1)S(1)} %collective-permute-done.10.refs_1_, bf16[96,1280]{1,0:T(8,128)(2,1)S(1)} %collective-permute-done.11.refs_2_, ...), custom_call_target="tpu_custom_call" | custom-call | tf_op jit(solution)/shard_map/place/pallas_call | solution.py:39
Async XLA Ops:
  0.0 1.4 %copy-start = (bf16[1,1,96,7680]{3,2,1,0:T(8,128)(2,1)S(1)}, bf16[1,1,96,7680]{3,2,1,0:T(8,128)(2,1)}, u32[]{:S(2)}) copy-start(bf16[1,1,96,7680]{3,2,1,0:T(8,128)(2,1)} %param.7) | copy-start | bytes 4423684
  1.4 6.8 %copy-start.1 = (bf16[1,1,96,7680]{3,2,1,0:T(8,128)(2,1)S(1)}, bf16[1,1,96,7680]{3,2,1,0:T(8,128)(2,1)}, u32[]{:S(2)}) copy-start(bf16[1,1,96,7680]{3,2,1,0:T(8,128)(2,1)} %param.7) | copy-start | bytes 4423684
  2.3 24.0 %collective-permute-start.4 = (bf16[96,1920]{1,0:T(8,128)(2,1)S(1)}, bf16[96,1920]{1,0:T(8,128)(2,1)S(1)}, u32[]{:S(2)}, u32[]{:S(2)}) collective-permute-start(bf16[96,1920]{1,0:T(8,128)(2,1)S(1)} %get-tuple-element.51), channel_id=1, source_target_pairs={{0,64},{64,128},{128,192},{192,0},{1,65},{65,129},{129,193},{193,1... | collective-permute-start | bytes 1105928 | tf_op jit(solution)/shard_map/ppermute | solution.py:339
  4.0 27.2 %collective-permute-start.5 = (bf16[96,1920]{1,0:T(8,128)(2,1)}, bf16[96,1920]{1,0:T(8,128)(2,1)S(1)}, u32[]{:S(2)}, u32[]{:S(2)}) collective-permute-start(bf16[96,1920]{1,0:T(8,128)(2,1)} %get-tuple-element.52), channel_id=1, source_target_pairs={{0,128},{64,192},{128,0},{192,64},{1,129},{65,193},{129,1},{193,65... | collective-permute-start | bytes 1105928 | tf_op jit(solution)/shard_map/ppermute | solution.py:339
  6.9 21.3 %copy-start.8 = (bf16[27,9216]{1,0:T(8,128)(2,1)S(1)}, bf16[27,9216]{1,0:T(8,128)(2,1)}, u32[]{:S(2)}) copy-start(bf16[27,9216]{1,0:T(8,128)(2,1)} %param.9) | copy-start | bytes 1492996
  6.9 24.3 %collective-permute-start.6 = (bf16[96,1920]{1,0:T(8,128)(2,1)}, bf16[96,1920]{1,0:T(8,128)(2,1)}, u32[]{:S(2)}, u32[]{:S(2)}) collective-permute-start(bf16[96,1920]{1,0:T(8,128)(2,1)} %get-tuple-element.53), channel_id=1, source_target_pairs={{0,192},{64,0},{128,64},{192,128},{1,193},{65,1},{129,65},{193,129... | collective-permute-start | bytes 1105928 | tf_op jit(solution)/shard_map/ppermute | solution.py:339
  9.5 5.2 %collective-permute-start = (bf16[96,320]{1,0:T(8,128)(2,1)S(1)}, bf16[96,320]{1,0:T(8,128)(2,1)S(1)}, u32[]{:S(2)}, u32[]{:S(2)}) collective-permute-start(bf16[96,320]{1,0:T(8,128)(2,1)S(1)} %get-tuple-element.44), channel_id=1, source_target_pairs={{0,8},{1,9},{2,10},{3,11},{4,12},{5,13},{6,14},{7,15},{8,16},{9,17... | collective-permute-start | bytes 184328 | tf_op jit(solution)/shard_map/ppermute | solution.py:348
  12.7 5.6 %collective-permute-start.1 = (bf16[96,320]{1,0:T(8,128)(2,1)S(1)}, bf16[96,320]{1,0:T(8,128)(2,1)S(1)}, u32[]{:S(2)}, u32[]{:S(2)}) collective-permute-start(bf16[96,320]{1,0:T(8,128)(2,1)S(1)} %get-tuple-element.45), channel_id=1, source_target_pairs={{0,56},{1,57},{2,58},{3,59},{4,60},{5,61},{6,62},{7,63},{8,0},{9,1... | collective-permute-start | bytes 184328 | tf_op jit(solution)/shard_map/ppermute | solution.py:348
  19.2 1.8 %collective-permute-start.3 = (bf16[96,256]{1,0:T(8,128)(2,1)S(1)}, bf16[96,256]{1,0:T(8,128)(2,1)S(1)}, u32[]{:S(2)}, u32[]{:S(2)}) collective-permute-start(bf16[96,256]{1,0:T(8,128)(2,1)S(1)} %get-tuple-element.48), channel_id=1, source_target_pairs={{0,7},{1,0},{2,1},{3,2},{4,3},{5,4},{6,5},{7,6},{8,15},{9,8},{10,9... | collective-permute-start | bytes 147464 | tf_op jit(solution)/shard_map/ppermute | solution.py:348
  19.2 3.5 %collective-permute-start.2 = (bf16[96,256]{1,0:T(8,128)(2,1)S(1)}, bf16[96,256]{1,0:T(8,128)(2,1)S(1)}, u32[]{:S(2)}, u32[]{:S(2)}) collective-permute-start(bf16[96,256]{1,0:T(8,128)(2,1)S(1)} %get-tuple-element.48), channel_id=1, source_target_pairs={{0,1},{1,2},{2,3},{3,4},{4,5},{5,6},{6,7},{7,0},{8,9},{9,10},{10,1... | collective-permute-start | bytes 147464 | tf_op jit(solution)/shard_map/ppermute | solution.py:348
  24.2 0.7 copy-start.3
  24.8 10.7 %collective-permute-start.7 = (bf16[96,768]{1,0:T(8,128)(2,1)}, bf16[96,768]{1,0:T(8,128)(2,1)}, u32[]{:S(2)}, u32[]{:S(2)}) collective-permute-start(bf16[96,768]{1,0:T(8,128)(2,1)} %get-tuple-element.57), channel_id=1, source_target_pairs={{0,64},{64,128},{128,192},{192,0},{1,65},{65,129},{129,193},{193,1... | collective-permute-start | bytes 442376 | tf_op jit(solution)/shard_map/ppermute | solution.py:339
  25.5 10.0 %collective-permute-start.8 = (bf16[96,768]{1,0:T(8,128)(2,1)}, bf16[96,768]{1,0:T(8,128)(2,1)}, u32[]{:S(2)}, u32[]{:S(2)}) collective-permute-start(bf16[96,768]{1,0:T(8,128)(2,1)} %get-tuple-element.58), channel_id=1, source_target_pairs={{0,128},{64,192},{128,0},{192,64},{1,129},{65,193},{129,1},{193,65... | collective-permute-start | bytes 442376 | tf_op jit(solution)/shard_map/ppermute | solution.py:339
  26.3 9.8 %collective-permute-start.9 = (bf16[96,768]{1,0:T(8,128)(2,1)}, bf16[96,768]{1,0:T(8,128)(2,1)}, u32[]{:S(2)}, u32[]{:S(2)}) collective-permute-start(bf16[96,768]{1,0:T(8,128)(2,1)} %get-tuple-element.59), channel_id=1, source_target_pairs={{0,192},{64,0},{128,64},{192,128},{1,193},{65,1},{129,65},{193,129... | collective-permute-start | bytes 442376 | tf_op jit(solution)/shard_map/ppermute | solution.py:339
  28.2 3.0 %copy-start.2 = (f32[96]{0:T(128)S(1)}, f32[96]{0:T(128)}, u32[]{:S(2)}) copy-start(f32[96]{0:T(128)} %param.8) | copy-start | bytes 1156
  30.6 5.6 %copy-start.4 = (bf16[96,768]{1,0:T(8,128)(2,1)S(1)}, bf16[96,768]{1,0:T(8,128)(2,1)}, u32[]{:S(2)}) copy-start(bf16[96,768]{1,0:T(8,128)(2,1)} %copy-done.3) | copy-start | bytes 442372
  30.6 5.6 %copy-start.5 = (f32[96]{0:T(128)S(1)}, f32[96]{0:T(128)}, u32[]{:S(2)}) copy-start(f32[96]{0:T(128)} %param.10) | copy-start | bytes 1156
  30.6 5.5 %copy-start.6 = (f32[96]{0:T(128)S(1)}, f32[96]{0:T(128)}, u32[]{:S(2)}) copy-start(f32[96]{0:T(128)} %param.11) | copy-start | bytes 1156
  30.6 5.5 %copy-start.7 = (f32[96]{0:T(128)S(1)}, f32[96]{0:T(128)}, u32[]{:S(2)}) copy-start(f32[96]{0:T(128)} %param.13) | copy-start | bytes 1156
  50.4 13.0 %collective-permute-start.10 = (bf16[96,1280]{1,0:T(8,128)(2,1)S(1)}, bf16[96,1280]{1,0:T(8,128)(2,1)S(1)}, u32[]{:S(2)}, u32[]{:S(2)}) collective-permute-start(bf16[96,1280]{1,0:T(8,128)(2,1)S(1)} %get-tuple-element.71), channel_id=1, source_target_pairs={{0,192},{64,0},{128,64},{192,128},{1,193},{65,1},{129,65},{193,129... | collective-permute-start | bytes 737288 | tf_op jit(solution)/shard_map/ppermute | solution.py:339
  52.9 10.5 %collective-permute-start.11 = (bf16[96,1280]{1,0:T(8,128)(2,1)S(1)}, bf16[96,1280]{1,0:T(8,128)(2,1)S(1)}, u32[]{:S(2)}, u32[]{:S(2)}) collective-permute-start(bf16[96,1280]{1,0:T(8,128)(2,1)S(1)} %get-tuple-element.72), channel_id=1, source_target_pairs={{0,128},{64,192},{128,0},{192,64},{1,129},{65,193},{129,1},{193,65... | collective-permute-start | bytes 737288 | tf_op jit(solution)/shard_map/ppermute | solution.py:339
  52.9 13.9 %collective-permute-start.12 = (bf16[96,1280]{1,0:T(8,128)(2,1)S(1)}, bf16[96,1280]{1,0:T(8,128)(2,1)S(1)}, u32[]{:S(2)}, u32[]{:S(2)}) collective-permute-start(bf16[96,1280]{1,0:T(8,128)(2,1)S(1)} %get-tuple-element.73), channel_id=1, source_target_pairs={{0,64},{64,128},{128,192},{192,0},{1,65},{65,129},{129,193},{193,1... | collective-permute-start | bytes 737288 | tf_op jit(solution)/shard_map/ppermute | solution.py:339
  66.8 6.2 %collective-permute-start.13 = (bf16[96,640]{1,0:T(8,128)(2,1)S(1)}, bf16[96,640]{1,0:T(8,128)(2,1)S(1)}, u32[]{:S(2)}, u32[]{:S(2)}) collective-permute-start(bf16[96,640]{1,0:T(8,128)(2,1)S(1)} %get-tuple-element.80), channel_id=1, source_target_pairs={{0,192},{64,0},{128,64},{192,128},{1,193},{65,1},{129,65},{193,129... | collective-permute-start | bytes 368648 | tf_op jit(solution)/shard_map/ppermute | solution.py:339
  67.7 7.6 %collective-permute-start.14 = (bf16[96,640]{1,0:T(8,128)(2,1)S(1)}, bf16[96,640]{1,0:T(8,128)(2,1)S(1)}, u32[]{:S(2)}, u32[]{:S(2)}) collective-permute-start(bf16[96,640]{1,0:T(8,128)(2,1)S(1)} %get-tuple-element.81), channel_id=1, source_target_pairs={{0,128},{64,192},{128,0},{192,64},{1,129},{65,193},{129,1},{193,65... | collective-permute-start | bytes 368648 | tf_op jit(solution)/shard_map/ppermute | solution.py:339
  68.1 7.8 %collective-permute-start.15 = (bf16[96,640]{1,0:T(8,128)(2,1)S(1)}, bf16[96,640]{1,0:T(8,128)(2,1)S(1)}, u32[]{:S(2)}, u32[]{:S(2)}) collective-permute-start(bf16[96,640]{1,0:T(8,128)(2,1)S(1)} %get-tuple-element.82), channel_id=1, source_target_pairs={{0,64},{64,128},{128,192},{192,0},{1,65},{65,129},{129,193},{193,1... | collective-permute-start | bytes 368648 | tf_op jit(solution)/shard_map/ppermute | solution.py:339
where the time goes:
time: 77.4 us; the launch traced here: 77.2 us
  Pallas kernels  33.5 us (43%)
  waiting for transfers between devices  20.4 us (26%)
  starting transfers between devices  18.5 us (24%)
  local copies, waits for them, and re-layouts  4.43 us (6%)
    pallas_call x9, Pallas kernels, call(): pl.pallas_call(kernel, out_shape=[jax.ShapeDtypeStruct(s, jnp.bfloat16) f...  33.5 us
    ppermute x12, starting transfers between devices, over_time(): return lax.ppermute(array, 'tm', pairs)  14.8 us
    ppermute x12, waiting for transfers between devices, over_time(): return lax.ppermute(array, 'tm', pairs)  11.8 us
    ppermute x4, waiting for transfers between devices, over_tiles(): return lax.ppermute(array, 'tile', pairs)  8.51 us
    ppermute x4, starting transfers between devices, over_tiles(): return lax.ppermute(array, 'tile', pairs)  3.72 us
    unnamed x18, local copies, waits for them, and re-layouts  2.06 us
    reshape x1, local copies, waits for them, and re-layouts, on_device(): second_weight.reshape(27, C, C)  1.72 us
  transfers between devices with their start and end apart: 16, of which 10 were waited for; matrix products, arithmetic and copies ran while one was open for 3% of the time, Pallas kernels for 22%

commit v1 on v0

--- a/solution.py
+++ b/solution.py
@@ -26,6 +26,7 @@
 RIM = 768
 SIDES = 256
 TILE = 256
+LIFT = 512
 
 eps = 1e-06
 MIB = 1024 * 1024
@@ -173,7 +174,6 @@
         self.out = up128(rows * PITCH)
         self.ext_at = first * PITCH // 128 * 128
         self.ext = up128((first + 2) * PITCH + self.hidden) - self.ext_at
-        self.placed = up128(first * PITCH + self.out) - self.ext_at
         self.held = max(self.hidden, up128(2 * PITCH + self.out))
 
 
@@ -185,19 +185,14 @@
 
 
 def block_kernel(first, rows, me_ref, exists, *refs):
-    acts, placed_in, r0, r1, r2, r3, w1, w2 = refs[:8]
+    placed, acts, r0, r1, r2, r3, w1, w2 = refs[:8]
     outs = refs[12:16]
-    ext, placed, rims, rim_acts, lifted, lifted2, parts, parts2, held, total, results, sems = refs[16:]
+    ext, rims, rim_acts, lifted, lifted2, parts, parts2, held, total, results, sems = refs[16:]
     size = Sizes(first, rows)
     me = me_ref[0]
-    copies = [
-        pltpu.make_async_copy(acts.at[:, :, pl.ds(size.ext_at, size.ext)], ext, sems.at[0]),
-        pltpu.make_async_copy(
-            placed_in.at[:, :, pl.ds(size.ext_at, size.placed)], placed, sems.at[1]
-        ),
-    ]
+    copies = [pltpu.make_async_copy(acts.at[:, :, pl.ds(size.ext_at, size.ext)], ext, sems.at[0])]
     for k, rim in enumerate((r0, r1, r2, r3)):
-        copies.append(pltpu.make_async_copy(rim, rims.at[frame_of(k, me)], sems.at[2 + k]))
+        copies.append(pltpu.make_async_copy(rim, rims.at[frame_of(k, me)], sems.at[1 + k]))
     for copy in copies:
         copy.start()
     g1, b1, g2, b2 = (upright(ref[...]) for ref in refs[8:12])
@@ -205,8 +200,8 @@
     for copy in copies:
         copy.wait()
 
-    def spans(lanes):
-        return [(at, min(TILE, lanes - at)) for at in range(0, lanes, TILE)]
+    def spans(lanes, step=TILE):
+        return [(at, min(step, lanes - at)) for at in range(0, lanes, step)]
 
     def lift(t):
         def rim_step():
@@ -231,7 +226,7 @@
 
         steps = [rim_step]
         steps += [functools.partial(row_step, i) for i in range(first, first + rows + 4)]
-        for at, wide in spans(size.hidden):
+        for at, wide in spans(size.hidden, LIFT):
             steps += [functools.partial(copy_step, di, at, wide) for di in range(3)]
         return steps
 
@@ -247,21 +242,34 @@
 
         return [functools.partial(step, at, wide) for at, wide in spans(lanes)]
 
-    def gathered(source, t, at, wide, lanes):
-        reach = min(wide + 128, lanes - at)
-        field = source[t % 2, 0:C, at : at + wide]
-        for dj in (1, 2):
-            part = source[t % 2, dj * C : (dj + 1) * C, at : at + reach]
-            field = field + pltpu.roll(part, reach - dj, 1)[:, :wide]
-        return field
+    lane = lax.broadcasted_iota(jnp.int32, (C, 128), 1)
+
+    def gathered(source, t, lanes):
+        moved = {}
+
+        def turned(dj, at):
+            if (dj, at) not in moved:
+                part = source[t % 2, dj * C : (dj + 1) * C, at : at + 128]
+                moved[dj, at] = pltpu.roll(part, 128 - dj, 1)
+            return moved[dj, at]
+
+        def block(at):
+            field = source[t % 2, 0:C, at : at + 128]
+            after = at + 128 if at + 128 < lanes else at
+            for dj in (1, 2):
+                field = field + jnp.where(lane < 128 - dj, turned(dj, at), turned(dj, after))
+            return field
+
+        return block
 
     def middle(t):
+        block = gathered(parts, t, size.hidden)
+
         def step(at, wide):
-            values = gathered(parts, t, at, wide, size.hidden) + b1
-            values = activated(values, g2) * mask[:, at : at + wide]
+            values = activated(block(at) + b1, g2) * mask[:, at : at + wide]
             held[t % 2, :, at : at + wide] = values.astype(jnp.bfloat16)
 
-        return [functools.partial(step, at, wide) for at, wide in spans(size.hidden)]
+        return [functools.partial(step, at, wide) for at, wide in spans(size.hidden, 128)]
 
     def lift2(t):
         def step(di, at, wide):
@@ -270,17 +278,21 @@
             to[...] = held[t % 2, :, start : start + wide]
 
         return [
-            functools.partial(step, di, at, wide) for at, wide in spans(size.out) for di in range(3)
+            functools.partial(step, di, at, wide)
+            for at, wide in spans(size.out, LIFT)
+            for di in range(3)
         ]
 
     def finish(t):
+        block = gathered(parts2, t, size.out)
+
         def step(at, wide):
-            start = first * PITCH - size.ext_at + at
-            values = gathered(parts2, t, at, wide, size.out) + b2
+            start = first * PITCH + at
+            values = block(at) + b2
             values = values + placed[t, :, start : start + wide].astype(jnp.float32)
             total[t % 2, :, at : at + wide] = values.astype(jnp.bfloat16)
 
-        return [functools.partial(step, at, min(wide, size.placed - at)) for at, wide in spans(size.out)]
+        return [functools.partial(step, at, wide) for at, wide in spans(size.out, 128)]
 
     def compact(t):
         def step(i):
@@ -294,6 +306,13 @@
 
     def second_products(t):
         return products(t, w2, lifted2, parts2, size.out)
+
+    def send(t):
+        for k in range(FRAMES):
+
+            @pl.when(frame_of(k, me) == t)
+            def _():
+                pltpu.make_async_copy(results.at[t], outs[k], sems.at[k]).start()
 
     for step in lift(0):
         step()
@@ -303,27 +322,28 @@
     together(second_products(0), lift2(1) + middle(2))
     together(first_products(3), lift2(2) + finish(0))
     together(second_products(1), middle(3) + compact(0))
+    send(0)
     together(second_products(2), lift2(3) + finish(1) + compact(1))
-    together(second_products(3), finish(2) + compact(2))
-    for step in finish(3) + compact(3):
+    send(1)
+    tiles, tail = second_products(3), finish(3)
+    ready = min(6, len(tiles) - 1)
+    together(tiles[:3], finish(2) + compact(2))
+    together(tiles[3:], tail[: 2 * ready - 1] if len(tiles) > 3 else [])
+    for step in (tail[2 * ready - 1 :] if len(tiles) > 3 else tail) + compact(3):
         step()
-    run_all(
-        [
-            pltpu.make_async_copy(results.at[frame_of(k, me)], outs[k], sems.at[k])
-            for k in range(FRAMES)
-        ]
-    )
-
-
-def place_kernel(me_ref, *refs):
-    pieces, out, sems = refs[:-2], refs[-2], refs[-1]
+    send(2)
+    send(3)
+    for k in range(FRAMES):
+        pltpu.make_async_copy(results.at[0], outs[k], sems.at[k]).wait()
+
+
+def place_kernel(first, rows, me_ref, *refs):
+    pieces, out, sems = refs[:FRAMES], refs[-2], refs[-1]
     copies = []
-    for part, (first, rows) in enumerate(PARTS):
-        for k in range(FRAMES):
-            start = pl.multiple_of(strip_at(k, me_ref[0]) + first * WT, 128)
-            place = out.at[:, pl.ds(start, rows * WT)]
-            n = part * FRAMES + k
-            copies.append(pltpu.make_async_copy(pieces[n], place, sems.at[n]))
+    for k in range(FRAMES):
+        start = pl.multiple_of(strip_at(k, me_ref[0]) + first * WT, 128)
+        place = out.at[:, pl.ds(start, rows * WT)]
+        copies.append(pltpu.make_async_copy(pieces[k], place, sems.at[k]))
     run_all(copies)
 
 
@@ -363,11 +383,10 @@
     return jnp.where(outside > 0, 0.0, 1.0)
 
 
-def block(first, rows, me, exists, sources, common):
+def block(first, rows, me, exists, placed, sources, common):
     size = Sizes(first, rows)
     scratch = [
         pltpu.VMEM((FRAMES, C, size.ext), jnp.bfloat16),
-        pltpu.VMEM((FRAMES, C, size.placed), jnp.bfloat16),
         pltpu.VMEM((FRAMES, C, RIM), jnp.bfloat16),
         pltpu.VMEM((FRAMES, C, RIM), jnp.bfloat16),
         pltpu.VMEM((FRAMES, 3 * C, size.hidden), jnp.bfloat16),
@@ -377,13 +396,13 @@
         pltpu.VMEM((2, C, size.held), jnp.bfloat16),
         pltpu.VMEM((2, C, size.out), jnp.bfloat16),
         pltpu.VMEM((FRAMES, C, rows * WT), jnp.bfloat16),
-        pltpu.SemaphoreType.DMA((6,)),
+        pltpu.SemaphoreType.DMA((5,)),
     ]
     return call(
         functools.partial(block_kernel, first, rows),
         [(C, rows * WT)] * FRAMES,
         scratch,
-        smem(me, exists) + anywhere(*sources) + vmem(*common),
+        smem(me, exists) + vmem(placed) + anywhere(*sources) + vmem(*common),
         out_space=pl.ANY,
         flops=2 * 27 * C * C * (2 * rows + 2) * WT * 3,
         mib=28,
@@ -405,16 +424,6 @@
     ).astype(jnp.int32)
     dma = pltpu.SemaphoreType.DMA
 
-    mains = call(
-        cut_kernel,
-        [(C, LANES)] * 3,
-        [dma((3,))],
-        smem(me) + anywhere(x),
-        out_space=pl.ANY,
-        moved=6 * C * LANES,
-        name="cut",
-    )
-    mains = [over_time(main, k + 1) for k, main in enumerate(mains)]
     top, bottom, quads = call(
         edge_kernel,
         [(C, 2 * WT)] * 2 + [(C, SIDES)],
@@ -423,6 +432,17 @@
         moved=2 * C * HT * WT,
         name="edges",
     )
+    top, bottom, me_cut = lax.optimization_barrier((top, bottom, me))
+    mains = call(
+        cut_kernel,
+        [(C, LANES)] * 3,
+        [dma((3,))],
+        smem(me_cut) + anywhere(x),
+        out_space=pl.ANY,
+        moved=6 * C * LANES,
+        name="cut",
+    )
+    mains = [over_time(main, k + 1) for k, main in enumerate(mains)]
     above = over_tiles(bottom, 1, 0)
     below = over_tiles(top, -1, 0)
     quads, rows = call(
@@ -464,25 +484,25 @@
         moved=8 * MIB,
         name="early",
     )
+    scales = [a[None] for a in (first_gain, first_bias, second_gain, second_bias)]
     pieces = []
-    scales = [a[None] for a in (first_gain, first_bias, second_gain, second_bias)]
+    me_block = me
     for first, rows in PARTS:
-        me_block = me if not pieces else pieces[-1][1]
-        outs = block(first, rows, me_block, exists, [acts, placed, *rims], [w1, w2, *scales])
-        if pieces:
-            outs, before = lax.optimization_barrier((outs, pieces[-1][0]))
-            pieces[-1] = (before, None)
+        outs = block(first, rows, me_block, exists, placed, [acts, *rims], [w1, w2, *scales])
         own, me_block = lax.optimization_barrier((outs[0], me))
-        pieces.append(([own] + [over_time(outs[k], -k) for k in (1, 2, 3)], me_block))
-    pieces = [piece for part, _ in pieces for piece in part]
-    (encoded,) = call(
-        place_kernel,
-        [(C, HT * WT)],
-        [dma((len(pieces),))],
-        smem(me) + anywhere(*pieces),
-        out_space=pl.ANY,
-        name="place",
-    )
+        pieces.append([own] + [over_time(outs[k], -k) for k in (1, 2, 3)])
+    encoded = []
+    for (first, rows), part in zip(PARTS, pieces):
+        encoded = call(
+            functools.partial(place_kernel, first, rows),
+            [(C, HT * WT)],
+            [dma((FRAMES,))],
+            smem(me) + anywhere(*part, *encoded),
+            out_space=pl.ANY,
+            input_output_aliases={1 + FRAMES: 0} if encoded else {},
+            name="place_%d" % first,
+        )
+    (encoded,) = encoded
     return encoded.reshape(1, 1, C, HT * WT)
 
 

time: 77.4 us -> 74.5 us (0.963)
  waiting for transfers between devices: 20.4 us -> 15.3 us
  starting transfers between devices: 18.5 us -> 21.1 us
    ppermute x12, waiting for transfers between devices: 11.8 us -> 6.76 us  [over_time(): return lax.ppermute(array, 'tm', pairs)]
    ppermute x12, starting transfers between devices: 14.8 us -> 17.4 us  [over_time(): return lax.ppermute(array, 'tm', pairs)]
    pallas_call x9 -> x10, Pallas kernels: 33.5 us -> 33 us  [call(): pl.pallas_call(kernel, out_shape=[jax.ShapeDtypeStruct(s, jnp.bfloat16) f...]
  transfers between devices with their start and end apart: 16 -> 16, of which waited for: 10 -> 9; matrix products, arithmetic and copies ran while one was open for 3% -> 3% of each run, Pallas kernels for 22% -> 22%
where the time goes in v1:
time: 74.5 us; the launch traced here: 74.2 us
  Pallas kernels  33 us (44%)
  starting transfers between devices  21.1 us (28%)
  waiting for transfers between devices  15.3 us (21%)
  local copies, waits for them, and re-layouts  4.51 us (6%)
    pallas_call x10, Pallas kernels, call(): pl.pallas_call(kernel, out_shape=[jax.ShapeDtypeStruct(s, jnp.bfloat16) f...  33 us
    ppermute x12, starting transfers between devices, over_time(): return lax.ppermute(array, 'tm', pairs)  17.4 us
    ppermute x4, waiting for transfers between devices, over_tiles(): return lax.ppermute(array, 'tile', pairs)  8.51 us
    ppermute x12, waiting for transfers between devices, over_time(): return lax.ppermute(array, 'tm', pairs)  6.76 us
    ppermute x4, starting transfers between devices, over_tiles(): return lax.ppermute(array, 'tile', pairs)  3.64 us
    unnamed x18, local copies, waits for them, and re-layouts  2.13 us
    reshape x1, local copies, waits for them, and re-layouts, on_device(): second_weight.reshape(27, C, C)  1.72 us
  transfers between devices with their start and end apart: 16, of which 9 were waited for; matrix products, arithmetic and copies ran while one was open for 3% of the time, Pallas kernels for 22%

profile of v1, /device:TPU:98, one launch (start us, length us, event | category | flops | bytes accessed | tf_op | source)
XLA Modules:
  0.0 74.2 jit_solution(9271573280777580606)
XLA Ops:
  0.0 0.0 copy-start
  0.0 1.4 %copy-done = bf16[1,1,96,7680]{3,2,1,0:T(8,128)(2,1)S(1)} copy-done((bf16[1,1,96,7680]{3,2,1,0:T(8,128)(2,1)S(1)}, bf16[1,1,96,7680]{3,2,1,0:T(8,128)(2,1)}, u32[]{:S(2)}) %copy-start) | copy-done | bytes 1474584
  1.4 0.0 copy-start.1
  1.4 1.3 %edges.1 = (bf16[96,320]{1,0:T(8,128)(2,1)S(1)}, bf16[96,320]{1,0:T(8,128)(2,1)S(1)}, bf16[96,256]{1,0:T(8,128)(2,1)S(1)}) custom-call(bf16[96,7680]{1,0:T(8,128)(2,1)S(1)} %bitcast.11), custom_call_target="tpu_custom_call" | custom-call | bytes 1474560 | tf_op jit(solution)/shard_map/edges/pallas_call | solution.py:40
  2.7 0.1 copy-done.1
  2.7 0.9 %cut.1 = (bf16[96,1920]{1,0:T(8,128)(2,1)S(1)}, bf16[96,1920]{1,0:T(8,128)(2,1)}, bf16[96,1920]{1,0:T(8,128)(2,1)}) custom-call(s32[1]{0:T(128)} %bitcast.me_ref, bf16[96,7680]{1,0:T(8,128)(2,1)S(1)} %bitcast.12), custom_call_target="tpu_custom_call" | custom-call | bytes 1105920 | tf_op jit(solution)/shard_map/cut/pallas_call | solution.py:40
  3.7 0.0 copy-start.8
  3.7 1.7 %collective-permute-start.4 = (bf16[96,1920]{1,0:T(8,128)(2,1)S(1)}, bf16[96,1920]{1,0:T(8,128)(2,1)S(1)}, u32[]{:S(2)}, u32[]{:S(2)}) collective-permute-start(bf16[96,1920]{1,0:T(8,128)(2,1)S(1)} %get-tuple-element.49), channel_id=1, source_target_pairs={{0,64},{64,128},{128,192},{192,0},{1,65},{65,129},{129,193},{193,1... | collective-permute-start | bytes 1105928 | tf_op jit(solution)/shard_map/ppermute | solution.py:359
  5.3 2.9 %collective-permute-start.5 = (bf16[96,1920]{1,0:T(8,128)(2,1)}, bf16[96,1920]{1,0:T(8,128)(2,1)S(1)}, u32[]{:S(2)}, u32[]{:S(2)}) collective-permute-start(bf16[96,1920]{1,0:T(8,128)(2,1)} %get-tuple-element.50), channel_id=1, source_target_pairs={{0,128},{64,192},{128,0},{192,64},{1,129},{65,193},{129,1},{193,65... | collective-permute-start | bytes 1105928 | tf_op jit(solution)/shard_map/ppermute | solution.py:359
  8.2 1.3 %collective-permute-start.6 = (bf16[96,1920]{1,0:T(8,128)(2,1)}, bf16[96,1920]{1,0:T(8,128)(2,1)}, u32[]{:S(2)}, u32[]{:S(2)}) collective-permute-start(bf16[96,1920]{1,0:T(8,128)(2,1)} %get-tuple-element.51), channel_id=1, source_target_pairs={{0,192},{64,0},{128,64},{192,128},{1,193},{65,1},{129,65},{193,129... | collective-permute-start | bytes 1105928 | tf_op jit(solution)/shard_map/ppermute | solution.py:359
  9.6 3.1 %collective-permute-start = (bf16[96,320]{1,0:T(8,128)(2,1)S(1)}, bf16[96,320]{1,0:T(8,128)(2,1)S(1)}, u32[]{:S(2)}, u32[]{:S(2)}) collective-permute-start(bf16[96,320]{1,0:T(8,128)(2,1)S(1)} %get-tuple-element.41), channel_id=1, source_target_pairs={{0,8},{1,9},{2,10},{3,11},{4,12},{5,13},{6,14},{7,15},{8,16},{9,17... | collective-permute-start | bytes 184328 | tf_op jit(solution)/shard_map/ppermute | solution.py:368
  12.7 0.0 collective-permute-start.1
  12.7 0.1 add_convert_fusion.exists
  12.8 1.9 %collective-permute-done.above = bf16[96,320]{1,0:T(8,128)(2,1)S(1)} collective-permute-done((bf16[96,320]{1,0:T(8,128)(2,1)S(1)}, bf16[96,320]{1,0:T(8,128)(2,1)S(1)}, u32[]{:S(2)}, u32[]{:S(2)}) %collective-permute-start) | collective-permute-done | bytes 61472 | tf_op jit(solution)/shard_map/ppermute | solution.py:368
  14.7 3.6 %collective-permute-done.1.below = bf16[96,320]{1,0:T(8,128)(2,1)S(1)} collective-permute-done((bf16[96,320]{1,0:T(8,128)(2,1)S(1)}, bf16[96,320]{1,0:T(8,128)(2,1)S(1)}, u32[]{:S(2)}, u32[]{:S(2)}) %collective-permute-start.1) | collective-permute-done | bytes 61472 | tf_op jit(solution)/shard_map/ppermute | solution.py:368
  18.3 0.9 %sides.1 = (bf16[96,256]{1,0:T(8,128)(2,1)S(1)}, bf16[4,96,640]{2,1,0:T(8,128)(2,1)S(1)}) custom-call(s32[1]{0:T(128)} %bitcast.me_ref, s32[4]{0:T(128)S(1)} %add_convert_fusion.exists, bf16[96,7680]{1,0:T(8,128)(2,1)S(1)} %bitcast.13, bf16[96,320]{1,0:T(8,128)(2,1)S(1)} %collective-permute-done.above, bf16[96,320]{1,0:T(8,128)(2,1)S(1)} %collective-permute-done.1.below, ...), custom_call_target="tpu_custom_call" | custom-call | bytes 196608 | tf_op jit(solution)/shard_map/sides/pallas_call | solution.py:40
  19.2 0.0 collective-permute-start.3
  19.2 0.5 collective-permute-start.2
  19.7 1.2 %collective-permute-done.3.from_right = bf16[96,256]{1,0:T(8,128)(2,1)S(1)} collective-permute-done((bf16[96,256]{1,0:T(8,128)(2,1)S(1)}, bf16[96,256]{1,0:T(8,128)(2,1)S(1)}, u32[]{:S(2)}, u32[]{:S(2)}) %collective-permute-start.3) | collective-permute-done | bytes 49184 | tf_op jit(solution)/shard_map/ppermute | solution.py:368
  20.9 1.8 %collective-permute-done.2.from_left = bf16[96,256]{1,0:T(8,128)(2,1)S(1)} collective-permute-done((bf16[96,256]{1,0:T(8,128)(2,1)S(1)}, bf16[96,256]{1,0:T(8,128)(2,1)S(1)}, u32[]{:S(2)}, u32[]{:S(2)}) %collective-permute-start.2) | collective-permute-done | bytes 49184 | tf_op jit(solution)/shard_map/ppermute | solution.py:368
  22.7 1.4 %rims.1 = (bf16[96,768]{1,0:T(8,128)(2,1)S(1)}, bf16[96,768]{1,0:T(8,128)(2,1)}, bf16[96,768]{1,0:T(8,128)(2,1)}, bf16[96,768]{1,0:T(8,128)(2,1)}) custom-call(s32[1]{0:T(128)} %bitcast.me_ref, s32[4]{0:T(128)S(1)} %add_convert_fusion.exists, bf16[4,96,640]{2,1,0:T(8,128)(2,1)S(1)} %get-tuple-element.44.rows, ...), custom_call_target="tpu_custom_call" | custom-call | bytes 589824 | tf_op jit(solution)/shard_map/rims/pallas_call | solution.py:40
  24.2 0.0 copy-start.3
  24.2 0.7 copy-done.3
  24.8 0.7 collective-permute-start.7
  25.5 0.8 %collective-permute-start.8 = (bf16[96,768]{1,0:T(8,128)(2,1)}, bf16[96,768]{1,0:T(8,128)(2,1)}, u32[]{:S(2)}, u32[]{:S(2)}) collective-permute-start(bf16[96,768]{1,0:T(8,128)(2,1)} %get-tuple-element.56), channel_id=1, source_target_pairs={{0,128},{64,192},{128,0},{192,64},{1,129},{65,193},{129,1},{193,65... | collective-permute-start | bytes 442376 | tf_op jit(solution)/shard_map/ppermute | solution.py:359
  26.3 0.0 collective-permute-done.4.m1
  26.3 1.9 %collective-permute-start.9 = (bf16[96,768]{1,0:T(8,128)(2,1)}, bf16[96,768]{1,0:T(8,128)(2,1)}, u32[]{:S(2)}, u32[]{:S(2)}) collective-permute-start(bf16[96,768]{1,0:T(8,128)(2,1)} %get-tuple-element.57), channel_id=1, source_target_pairs={{0,192},{64,0},{128,64},{192,128},{1,193},{65,1},{129,65},{193,129... | collective-permute-start | bytes 442376 | tf_op jit(solution)/shard_map/ppermute | solution.py:359
  28.2 0.0 copy-done.8
  28.2 0.7 reshape.17.first
  28.8 0.0 copy-start.2
  28.9 1.7 %reshape.18.second = bf16[27,96,96]{2,1,0:T(8,128)(2,1)S(1)} reshape(bf16[27,9216]{1,0:T(8,128)(2,1)} %param.12) | data formatting | bytes 995328 | tf_op jit(solution)/shard_map/reshape | solution.py:474
  30.6 0.5 weights.1
  31.1 0.0 copy-start.4
  31.1 0.0 copy-start.5
  31.1 0.0 copy-start.6
  31.1 0.0 copy-start.7
  31.1 0.0 collective-permute-done.5.m2
  31.2 0.0 collective-permute-done.6.m3
  31.2 0.0 copy-done.2
  31.2 3.4 %early.1 = (bf16[4,96,2688]{2,1,0:T(8,128)(2,1)S(1)}, bf16[4,96,2176]{2,1,0:T(8,128)(2,1)S(1)}) custom-call(s32[1]{0:T(128)} %bitcast.me_ref, f32[1,96]{1,0:T(1,128)S(1)} %bitcast.15, bf16[96,7680]{1,0:T(8,128)(2,1)S(1)} %bitcast.14, bf16[96,1920]{1,0:T(8,128)(2,1)S(1)} %collective-permute-done.4.m1, bf16[96,1920]{1,0:T(8,128)(2,1)S(1)} %collective-permute-done.5.m2, ...), custom_call_target="tpu_custom_call" | custom-call | bytes 8388608 | tf_op jit(solution)/shard_map/early/pallas_call | solution.py:40
  34.6 0.9 %collective-permute-done.7.refs_3_ = bf16[96,768]{1,0:T(8,128)(2,1)} collective-permute-done((bf16[96,768]{1,0:T(8,128)(2,1)}, bf16[96,768]{1,0:T(8,128)(2,1)}, u32[]{:S(2)}, u32[]{:S(2)}) %collective-permute-start.7) | collective-permute-done | bytes 147488 | tf_op jit(solution)/shard_map/ppermute | solution.py:359
  35.5 0.0 collective-permute-done.8.refs_4_
  35.5 0.6 collective-permute-done.9.refs_5_
  36.1 0.0 copy-done.4
  36.1 0.0 copy-done.5
  36.1 0.0 copy-done.6
  36.1 0.0 copy-done.7
  36.1 13.5 %block_0.1 = (bf16[96,1280]{1,0:T(8,128)(2,1)S(1)}, bf16[96,1280]{1,0:T(8,128)(2,1)S(1)}, bf16[96,1280]{1,0:T(8,128)(2,1)S(1)}, bf16[96,1280]{1,0:T(8,128)(2,1)S(1)}) custom-call(s32[1]{0:T(128)} %bitcast.me_ref, s32[4]{0:T(128)S(1)} %add_convert_fusion.exists, bf16[4,96,2176]{2,1,0:T(8,128)(2,1)S(1)} %get-tuple-element.52.refs_0_, ...), custom_call_target="tpu_custom_call" | custom-call | flops 4299816960 | bytes 8388608 | tf_op jit(solution)/shard_map/block_0/pallas_call | solution.py:40
  49.6 2.5 %collective-permute-start.13 = (bf16[96,1280]{1,0:T(8,128)(2,1)S(1)}, bf16[96,1280]{1,0:T(8,128)(2,1)S(1)}, u32[]{:S(2)}, u32[]{:S(2)}) collective-permute-start(bf16[96,1280]{1,0:T(8,128)(2,1)S(1)} %get-tuple-element.70), channel_id=1, source_target_pairs={{0,192},{64,0},{128,64},{192,128},{1,193},{65,1},{129,65},{193,129... | collective-permute-start | bytes 737288 | tf_op jit(solution)/shard_map/ppermute | solution.py:359
  52.2 0.0 collective-permute-start.14
  52.2 0.9 %collective-permute-start.15 = (bf16[96,1280]{1,0:T(8,128)(2,1)S(1)}, bf16[96,1280]{1,0:T(8,128)(2,1)S(1)}, u32[]{:S(2)}, u32[]{:S(2)}) collective-permute-start(bf16[96,1280]{1,0:T(8,128)(2,1)S(1)} %get-tuple-element.72), channel_id=1, source_target_pairs={{0,64},{64,128},{128,192},{192,0},{1,65},{65,129},{129,193},{193,1... | collective-permute-start | bytes 737288 | tf_op jit(solution)/shard_map/ppermute | solution.py:359
  53.1 9.2 %block_8.1 = (bf16[96,640]{1,0:T(8,128)(2,1)S(1)}, bf16[96,640]{1,0:T(8,128)(2,1)S(1)}, bf16[96,640]{1,0:T(8,128)(2,1)S(1)}, bf16[96,640]{1,0:T(8,128)(2,1)S(1)}) custom-call(s32[1]{0:T(128)} %bitcast.me_ref, s32[4]{0:T(128)S(1)} %add_convert_fusion.exists, bf16[4,96,2176]{2,1,0:T(8,128)(2,1)S(1)} %get-tuple-element.52.refs_0_, ...), custom_call_target="tpu_custom_call" | custom-call | flops 2388787200 | bytes 8388608 | tf_op jit(solution)/shard_map/block_8/pallas_call | solution.py:40
  62.4 2.4 %collective-permute-start.10 = (bf16[96,640]{1,0:T(8,128)(2,1)S(1)}, bf16[96,640]{1,0:T(8,128)(2,1)S(1)}, u32[]{:S(2)}, u32[]{:S(2)}) collective-permute-start(bf16[96,640]{1,0:T(8,128)(2,1)S(1)} %get-tuple-element.66), channel_id=1, source_target_pairs={{0,192},{64,0},{128,64},{192,128},{1,193},{65,1},{129,65},{193,129... | collective-permute-start | bytes 368648 | tf_op jit(solution)/shard_map/ppermute | solution.py:359
  64.8 2.3 %collective-permute-start.11 = (bf16[96,640]{1,0:T(8,128)(2,1)S(1)}, bf16[96,640]{1,0:T(8,128)(2,1)S(1)}, u32[]{:S(2)}, u32[]{:S(2)}) collective-permute-start(bf16[96,640]{1,0:T(8,128)(2,1)S(1)} %get-tuple-element.67), channel_id=1, source_target_pairs={{0,128},{64,192},{128,0},{192,64},{1,129},{65,193},{129,1},{193,65... | collective-permute-start | bytes 368648 | tf_op jit(solution)/shard_map/ppermute | solution.py:359
  67.1 0.0 collective-permute-done.13.refs_1_
  67.1 0.0 collective-permute-start.12
  67.1 0.0 collective-permute-done.14.refs_2_
  67.1 0.0 collective-permute-done.15.refs_3_
  67.1 1.0 %place_0.1.refs_4_ = bf16[96,7680]{1,0:T(8,128)(2,1)} custom-call(s32[1]{0:T(128)} %bitcast.me_ref, bf16[96,1280]{1,0:T(8,128)(2,1)S(1)} %get-tuple-element.69.refs_0_, bf16[96,1280]{1,0:T(8,128)(2,1)S(1)} %collective-permute-done.13.refs_1_, bf16[96,1280]{1,0:T(8,128)(2,1)S(1)} %collective-permute-done.14.refs_2_, ...), custom_call_target="tpu_custom_call" | custom-call | tf_op jit(solution)/shard_map/place_0/pallas_call | solution.py:40
  68.1 1.4 %collective-permute-done.10.refs_1_ = bf16[96,640]{1,0:T(8,128)(2,1)S(1)} collective-permute-done((bf16[96,640]{1,0:T(8,128)(2,1)S(1)}, bf16[96,640]{1,0:T(8,128)(2,1)S(1)}, u32[]{:S(2)}, u32[]{:S(2)}) %collective-permute-start.10) | collective-permute-done | bytes 122912 | tf_op jit(solution)/shard_map/ppermute | solution.py:359
  69.4 2.5 %collective-permute-done.11.refs_2_ = bf16[96,640]{1,0:T(8,128)(2,1)S(1)} collective-permute-done((bf16[96,640]{1,0:T(8,128)(2,1)S(1)}, bf16[96,640]{1,0:T(8,128)(2,1)S(1)}, u32[]{:S(2)}, u32[]{:S(2)}) %collective-permute-start.11) | collective-permute-done | bytes 122912 | tf_op jit(solution)/shard_map/ppermute | solution.py:359
  71.9 1.4 %collective-permute-done.12.refs_3_ = bf16[96,640]{1,0:T(8,128)(2,1)S(1)} collective-permute-done((bf16[96,640]{1,0:T(8,128)(2,1)S(1)}, bf16[96,640]{1,0:T(8,128)(2,1)S(1)}, u32[]{:S(2)}, u32[]{:S(2)}) %collective-permute-start.12) | collective-permute-done | bytes 122912 | tf_op jit(solution)/shard_map/ppermute | solution.py:359
  73.3 0.8 %place_8.1 = bf16[96,7680]{1,0:T(8,128)(2,1)} custom-call(s32[1]{0:T(128)} %bitcast.me_ref, bf16[96,640]{1,0:T(8,128)(2,1)S(1)} %get-tuple-element.65.refs_0_, bf16[96,640]{1,0:T(8,128)(2,1)S(1)} %collective-permute-done.10.refs_1_, bf16[96,640]{1,0:T(8,128)(2,1)S(1)} %collective-permute-done.11.refs_2_, ...), custom_call_target="tpu_custom_call", output_to_operand_aliasing={{}: (5, {})} | custom-call | tf_op jit(solution)/shard_map/place_8/pallas_call | solution.py:40
Async XLA Ops:
  0.0 1.4 %copy-start = (bf16[1,1,96,7680]{3,2,1,0:T(8,128)(2,1)S(1)}, bf16[1,1,96,7680]{3,2,1,0:T(8,128)(2,1)}, u32[]{:S(2)}) copy-start(bf16[1,1,96,7680]{3,2,1,0:T(8,128)(2,1)} %param.7) | copy-start | bytes 4423684
  1.4 1.4 %copy-start.1 = (bf16[1,1,96,7680]{3,2,1,0:T(8,128)(2,1)S(1)}, bf16[1,1,96,7680]{3,2,1,0:T(8,128)(2,1)}, u32[]{:S(2)}) copy-start(bf16[1,1,96,7680]{3,2,1,0:T(8,128)(2,1)} %param.7) | copy-start | bytes 4423684
  3.7 24.5 %copy-start.8 = (bf16[27,9216]{1,0:T(8,128)(2,1)S(1)}, bf16[27,9216]{1,0:T(8,128)(2,1)}, u32[]{:S(2)}) copy-start(bf16[27,9216]{1,0:T(8,128)(2,1)} %param.9) | copy-start | bytes 1492996
  3.7 22.6 %collective-permute-start.4 = (bf16[96,1920]{1,0:T(8,128)(2,1)S(1)}, bf16[96,1920]{1,0:T(8,128)(2,1)S(1)}, u32[]{:S(2)}, u32[]{:S(2)}) collective-permute-start(bf16[96,1920]{1,0:T(8,128)(2,1)S(1)} %get-tuple-element.49), channel_id=1, source_target_pairs={{0,64},{64,128},{128,192},{192,0},{1,65},{65,129},{129,193},{193,1... | collective-permute-start | bytes 1105928 | tf_op jit(solution)/shard_map/ppermute | solution.py:359
  5.3 25.8 %collective-permute-start.5 = (bf16[96,1920]{1,0:T(8,128)(2,1)}, bf16[96,1920]{1,0:T(8,128)(2,1)S(1)}, u32[]{:S(2)}, u32[]{:S(2)}) collective-permute-start(bf16[96,1920]{1,0:T(8,128)(2,1)} %get-tuple-element.50), channel_id=1, source_target_pairs={{0,128},{64,192},{128,0},{192,64},{1,129},{65,193},{129,1},{193,65... | collective-permute-start | bytes 1105928 | tf_op jit(solution)/shard_map/ppermute | solution.py:359
  8.2 22.9 %collective-permute-start.6 = (bf16[96,1920]{1,0:T(8,128)(2,1)}, bf16[96,1920]{1,0:T(8,128)(2,1)}, u32[]{:S(2)}, u32[]{:S(2)}) collective-permute-start(bf16[96,1920]{1,0:T(8,128)(2,1)} %get-tuple-element.51), channel_id=1, source_target_pairs={{0,192},{64,0},{128,64},{192,128},{1,193},{65,1},{129,65},{193,129... | collective-permute-start | bytes 1105928 | tf_op jit(solution)/shard_map/ppermute | solution.py:359
  9.6 5.1 %collective-permute-start = (bf16[96,320]{1,0:T(8,128)(2,1)S(1)}, bf16[96,320]{1,0:T(8,128)(2,1)S(1)}, u32[]{:S(2)}, u32[]{:S(2)}) collective-permute-start(bf16[96,320]{1,0:T(8,128)(2,1)S(1)} %get-tuple-element.41), channel_id=1, source_target_pairs={{0,8},{1,9},{2,10},{3,11},{4,12},{5,13},{6,14},{7,15},{8,16},{9,17... | collective-permute-start | bytes 184328 | tf_op jit(solution)/shard_map/ppermute | solution.py:368
  12.7 5.6 %collective-permute-start.1 = (bf16[96,320]{1,0:T(8,128)(2,1)S(1)}, bf16[96,320]{1,0:T(8,128)(2,1)S(1)}, u32[]{:S(2)}, u32[]{:S(2)}) collective-permute-start(bf16[96,320]{1,0:T(8,128)(2,1)S(1)} %get-tuple-element.42), channel_id=1, source_target_pairs={{0,56},{1,57},{2,58},{3,59},{4,60},{5,61},{6,62},{7,63},{8,0},{9,1... | collective-permute-start | bytes 184328 | tf_op jit(solution)/shard_map/ppermute | solution.py:368
  19.2 1.8 %collective-permute-start.3 = (bf16[96,256]{1,0:T(8,128)(2,1)S(1)}, bf16[96,256]{1,0:T(8,128)(2,1)S(1)}, u32[]{:S(2)}, u32[]{:S(2)}) collective-permute-start(bf16[96,256]{1,0:T(8,128)(2,1)S(1)} %get-tuple-element.45), channel_id=1, source_target_pairs={{0,7},{1,0},{2,1},{3,2},{4,3},{5,4},{6,5},{7,6},{8,15},{9,8},{10,9... | collective-permute-start | bytes 147464 | tf_op jit(solution)/shard_map/ppermute | solution.py:368
  19.2 3.5 %collective-permute-start.2 = (bf16[96,256]{1,0:T(8,128)(2,1)S(1)}, bf16[96,256]{1,0:T(8,128)(2,1)S(1)}, u32[]{:S(2)}, u32[]{:S(2)}) collective-permute-start(bf16[96,256]{1,0:T(8,128)(2,1)S(1)} %get-tuple-element.45), channel_id=1, source_target_pairs={{0,1},{1,2},{2,3},{3,4},{4,5},{5,6},{6,7},{7,0},{8,9},{9,10},{10,1... | collective-permute-start | bytes 147464 | tf_op jit(solution)/shard_map/ppermute | solution.py:368
  24.2 0.7 copy-start.3
  24.8 10.7 %collective-permute-start.7 = (bf16[96,768]{1,0:T(8,128)(2,1)}, bf16[96,768]{1,0:T(8,128)(2,1)}, u32[]{:S(2)}, u32[]{:S(2)}) collective-permute-start(bf16[96,768]{1,0:T(8,128)(2,1)} %get-tuple-element.55), channel_id=1, source_target_pairs={{0,64},{64,128},{128,192},{192,0},{1,65},{65,129},{129,193},{193,1... | collective-permute-start | bytes 442376 | tf_op jit(solution)/shard_map/ppermute | solution.py:359
  25.5 10.0 %collective-permute-start.8 = (bf16[96,768]{1,0:T(8,128)(2,1)}, bf16[96,768]{1,0:T(8,128)(2,1)}, u32[]{:S(2)}, u32[]{:S(2)}) collective-permute-start(bf16[96,768]{1,0:T(8,128)(2,1)} %get-tuple-element.56), channel_id=1, source_target_pairs={{0,128},{64,192},{128,0},{192,64},{1,129},{65,193},{129,1},{193,65... | collective-permute-start | bytes 442376 | tf_op jit(solution)/shard_map/ppermute | solution.py:359
  26.3 9.8 %collective-permute-start.9 = (bf16[96,768]{1,0:T(8,128)(2,1)}, bf16[96,768]{1,0:T(8,128)(2,1)}, u32[]{:S(2)}, u32[]{:S(2)}) collective-permute-start(bf16[96,768]{1,0:T(8,128)(2,1)} %get-tuple-element.57), channel_id=1, source_target_pairs={{0,192},{64,0},{128,64},{192,128},{1,193},{65,1},{129,65},{193,129... | collective-permute-start | bytes 442376 | tf_op jit(solution)/shard_map/ppermute | solution.py:359
  28.8 2.3 %copy-start.2 = (f32[96]{0:T(128)S(1)}, f32[96]{0:T(128)}, u32[]{:S(2)}) copy-start(f32[96]{0:T(128)} %param.8) | copy-start | bytes 1156
  31.1 5.0 %copy-start.4 = (bf16[96,768]{1,0:T(8,128)(2,1)S(1)}, bf16[96,768]{1,0:T(8,128)(2,1)}, u32[]{:S(2)}) copy-start(bf16[96,768]{1,0:T(8,128)(2,1)} %copy-done.3) | copy-start | bytes 442372
  31.1 5.0 %copy-start.5 = (f32[96]{0:T(128)S(1)}, f32[96]{0:T(128)}, u32[]{:S(2)}) copy-start(f32[96]{0:T(128)} %param.10) | copy-start | bytes 1156
  31.1 5.0 %copy-start.6 = (f32[96]{0:T(128)S(1)}, f32[96]{0:T(128)}, u32[]{:S(2)}) copy-start(f32[96]{0:T(128)} %param.11) | copy-start | bytes 1156
  31.1 5.0 %copy-start.7 = (f32[96]{0:T(128)S(1)}, f32[96]{0:T(128)}, u32[]{:S(2)}) copy-start(f32[96]{0:T(128)} %param.13) | copy-start | bytes 1156
  49.6 17.4 %collective-permute-start.13 = (bf16[96,1280]{1,0:T(8,128)(2,1)S(1)}, bf16[96,1280]{1,0:T(8,128)(2,1)S(1)}, u32[]{:S(2)}, u32[]{:S(2)}) collective-permute-start(bf16[96,1280]{1,0:T(8,128)(2,1)S(1)} %get-tuple-element.70), channel_id=1, source_target_pairs={{0,192},{64,0},{128,64},{192,128},{1,193},{65,1},{129,65},{193,129... | collective-permute-start | bytes 737288 | tf_op jit(solution)/shard_map/ppermute | solution.py:359
  52.2 14.9 %collective-permute-start.14 = (bf16[96,1280]{1,0:T(8,128)(2,1)S(1)}, bf16[96,1280]{1,0:T(8,128)(2,1)S(1)}, u32[]{:S(2)}, u32[]{:S(2)}) collective-permute-start(bf16[96,1280]{1,0:T(8,128)(2,1)S(1)} %get-tuple-element.71), channel_id=1, source_target_pairs={{0,128},{64,192},{128,0},{192,64},{1,129},{65,193},{129,1},{193,65... | collective-permute-start | bytes 737288 | tf_op jit(solution)/shard_map/ppermute | solution.py:359
  52.2 14.9 %collective-permute-start.15 = (bf16[96,1280]{1,0:T(8,128)(2,1)S(1)}, bf16[96,1280]{1,0:T(8,128)(2,1)S(1)}, u32[]{:S(2)}, u32[]{:S(2)}) collective-permute-start(bf16[96,1280]{1,0:T(8,128)(2,1)S(1)} %get-tuple-element.72), channel_id=1, source_target_pairs={{0,64},{64,128},{128,192},{192,0},{1,65},{65,129},{129,193},{193,1... | collective-permute-start | bytes 737288 | tf_op jit(solution)/shard_map/ppermute | solution.py:359
  62.4 7.0 %collective-permute-start.10 = (bf16[96,640]{1,0:T(8,128)(2,1)S(1)}, bf16[96,640]{1,0:T(8,128)(2,1)S(1)}, u32[]{:S(2)}, u32[]{:S(2)}) collective-permute-start(bf16[96,640]{1,0:T(8,128)(2,1)S(1)} %get-tuple-element.66), channel_id=1, source_target_pairs={{0,192},{64,0},{128,64},{192,128},{1,193},{65,1},{129,65},{193,129... | collective-permute-start | bytes 368648 | tf_op jit(solution)/shard_map/ppermute | solution.py:359
  64.8 7.1 %collective-permute-start.11 = (bf16[96,640]{1,0:T(8,128)(2,1)S(1)}, bf16[96,640]{1,0:T(8,128)(2,1)S(1)}, u32[]{:S(2)}, u32[]{:S(2)}) collective-permute-start(bf16[96,640]{1,0:T(8,128)(2,1)S(1)} %get-tuple-element.67), channel_id=1, source_target_pairs={{0,128},{64,192},{128,0},{192,64},{1,129},{65,193},{129,1},{193,65... | collective-permute-start | bytes 368648 | tf_op jit(solution)/shard_map/ppermute | solution.py:359
  67.1 6.2 %collective-permute-start.12 = (bf16[96,640]{1,0:T(8,128)(2,1)S(1)}, bf16[96,640]{1,0:T(8,128)(2,1)S(1)}, u32[]{:S(2)}, u32[]{:S(2)}) collective-permute-start(bf16[96,640]{1,0:T(8,128)(2,1)S(1)} %get-tuple-element.68), channel_id=1, source_target_pairs={{0,64},{64,128},{128,192},{192,0},{1,65},{65,129},{129,193},{193,1... | collective-permute-start | bytes 368648 | tf_op jit(solution)/shard_map/ppermute | solution.py:359

commit v2 on v1

--- a/solution.py
+++ b/solution.py
@@ -26,7 +26,8 @@
 RIM = 768
 SIDES = 256
 TILE = 256
-LIFT = 512
+LIFT = 1024
+CARRY = 384
 
 eps = 1e-06
 MIB = 1024 * 1024
@@ -170,11 +171,18 @@
 
 class Sizes:
     def __init__(self, first, rows):
-        self.hidden = up128((rows + 2) * PITCH)
+        self.taken = 2 if first else 0
+        self.start = first + self.taken
+        self.hidden_rows = rows + 2 - self.taken
+        self.hidden = up128(self.hidden_rows * PITCH)
         self.out = up128(rows * PITCH)
-        self.ext_at = first * PITCH // 128 * 128
-        self.ext = up128((first + 2) * PITCH + self.hidden) - self.ext_at
-        self.held = max(self.hidden, up128(2 * PITCH + self.out))
+        self.ext_at = self.start * PITCH // 128 * 128
+        self.ext = min(up128((self.start + 2) * PITCH + self.hidden), EXT) - self.ext_at
+        self.held_new = CARRY if first else 0
+        self.held_at = self.held_new - self.taken * PITCH
+        self.held = up128(
+            max(self.held_new + self.hidden, self.held_at + 2 * PITCH + self.out)
+        )
 
 
 def together(tiles, tasks):
@@ -186,8 +194,8 @@
 
 def block_kernel(first, rows, me_ref, exists, *refs):
     placed, acts, r0, r1, r2, r3, w1, w2 = refs[:8]
-    outs = refs[12:16]
-    ext, rims, rim_acts, lifted, lifted2, parts, parts2, held, total, results, sems = refs[16:]
+    outs, carry = (refs[13:17], refs[12]) if first else (refs[12:16], refs[16])
+    ext, rims, rim_acts, lifted, lifted2, parts, parts2, held, total, results, sems = refs[17:]
     size = Sizes(first, rows)
     me = me_ref[0]
     copies = [pltpu.make_async_copy(acts.at[:, :, pl.ds(size.ext_at, size.ext)], ext, sems.at[0])]
@@ -204,8 +212,9 @@
         return [(at, min(step, lanes - at)) for at in range(0, lanes, step)]
 
     def lift(t):
-        def rim_step():
-            rim_acts[t] = activated(rims[t].astype(jnp.float32), g1).astype(jnp.bfloat16)
+        def rim_step(at, end):
+            values = activated(rims[t, :, at:end].astype(jnp.float32), g1)
+            rim_acts[t, :, at:end] = values.astype(jnp.bfloat16)
 
         def row_step(i):
             at = i * PITCH + 2 - size.ext_at
@@ -215,17 +224,21 @@
                 near = (i - STRIP) * WT
                 ext[t, :, at : at + WT] = rim_acts[t, :, near : near + WT]
             side = 4 * WT + 4 * i
-            if i == first:
+            if i == size.start:
                 ext[t, :, at - 2 : at] = rim_acts[t, :, side : side + 2]
             last = 2 if i == first + rows + 3 else 4
             ext[t, :, at + WT : at + WT + last] = rim_acts[t, :, side + 2 : side + 2 + last]
 
         def copy_step(di, at, wide):
-            start = (first + di) * PITCH - size.ext_at + at
+            start = (size.start + di) * PITCH - size.ext_at + at
+            wide = min(wide, size.ext - start)
             lifted[t, di * C : (di + 1) * C, at : at + wide] = ext[t, :, start : start + wide]
 
-        steps = [rim_step]
-        steps += [functools.partial(row_step, i) for i in range(first, first + rows + 4)]
+        needed = [(0, 384), (640, RIM)] if first == 0 else [(256, RIM)]
+        if first == 0 and first + rows == STRIP:
+            needed = [(0, RIM)]
+        steps = [functools.partial(rim_step, at, end) for at, end in needed]
+        steps += [functools.partial(row_step, i) for i in range(size.start, first + rows + 4)]
         for at, wide in spans(size.hidden, LIFT):
             steps += [functools.partial(copy_step, di, at, wide) for di in range(3)]
         return steps
@@ -267,13 +280,22 @@
 
         def step(at, wide):
             values = activated(block(at) + b1, g2) * mask[:, at : at + wide]
-            held[t % 2, :, at : at + wide] = values.astype(jnp.bfloat16)
-
-        return [functools.partial(step, at, wide) for at, wide in spans(size.hidden, 128)]
+            values = values.astype(jnp.bfloat16)
+            held[t % 2, :, size.held_new + at : size.held_new + at + wide] = values
+
+        def give():
+            end = size.hidden_rows * PITCH
+            carry[t] = held[t % 2, :, end - CARRY : end]
+
+        def take():
+            held[t % 2, :, :CARRY] = carry[t]
+
+        steps = [functools.partial(step, at, wide) for at, wide in spans(size.hidden, 128)]
+        return [take] + steps if first else steps + [give]
 
     def lift2(t):
         def step(di, at, wide):
-            start = di * PITCH + at
+            start = size.held_at + di * PITCH + at
             to = lifted2.at[t, pl.ds(di * C, C), pl.ds(at, wide)]
             to[...] = held[t % 2, :, start : start + wide]
 
@@ -369,21 +391,22 @@
 
 
 def inside(first, rows, me, exists):
-    lane = lax.broadcasted_iota(jnp.int32, (1, Sizes(first, rows).hidden), 1)
+    size = Sizes(first, rows)
+    lane = lax.broadcasted_iota(jnp.int32, (1, size.hidden), 1)
     outside = jnp.zeros(lane.shape, jnp.int32)
     if first == 0:
         absent = jnp.where(jnp.logical_or(me > 0, exists[0] > 0), 0, 1)
         outside += jnp.where(lane < PITCH, absent, 0)
     if first + rows == STRIP:
         absent = jnp.where(jnp.logical_or(me < FRAMES - 1, exists[1] > 0), 0, 1)
-        outside += jnp.where(lane >= (rows + 1) * PITCH, absent, 0)
-    for i in range(rows + 2):
+        outside += jnp.where(lane >= (size.hidden_rows - 1) * PITCH, absent, 0)
+    for i in range(size.hidden_rows):
         outside += jnp.where(lane == i * PITCH, 1 - exists[2], 0)
         outside += jnp.where(lane == i * PITCH + WT + 1, 1 - exists[3], 0)
     return jnp.where(outside > 0, 0.0, 1.0)
 
 
-def block(first, rows, me, exists, placed, sources, common):
+def block(first, rows, me, exists, placed, carry, sources, common):
     size = Sizes(first, rows)
     scratch = [
         pltpu.VMEM((FRAMES, C, size.ext), jnp.bfloat16),
@@ -400,10 +423,10 @@
     ]
     return call(
         functools.partial(block_kernel, first, rows),
-        [(C, rows * WT)] * FRAMES,
+        [(C, rows * WT)] * FRAMES + ([] if first else [(FRAMES, C, CARRY)]),
         scratch,
-        smem(me, exists) + vmem(placed) + anywhere(*sources) + vmem(*common),
-        out_space=pl.ANY,
+        smem(me, exists) + vmem(placed) + anywhere(*sources) + vmem(*common, *carry),
+        out_space=(pl.ANY,) * FRAMES + (() if first else (pltpu.VMEM,)),
         flops=2 * 27 * C * C * (2 * rows + 2) * WT * 3,
         mib=28,
         moved=8 * MIB,
@@ -486,10 +509,11 @@
     )
     scales = [a[None] for a in (first_gain, first_bias, second_gain, second_bias)]
     pieces = []
-    me_block = me
+    carry = []
     for first, rows in PARTS:
-        outs = block(first, rows, me_block, exists, placed, [acts, *rims], [w1, w2, *scales])
-        own, me_block = lax.optimization_barrier((outs[0], me))
+        common = [w1, w2, *scales]
+        outs = block(first, rows, me, exists, placed, carry, [acts, *rims], common)
+        own, *carry = lax.optimization_barrier((outs[0], *outs[FRAMES:]))
         pieces.append([own] + [over_time(outs[k], -k) for k in (1, 2, 3)])
     encoded = []
     for (first, rows), part in zip(PARTS, pieces):

time: 74.5 us -> 73.6 us (0.988)
  Pallas kernels: 33 us -> 32.2 us
    pallas_call x10, Pallas kernels: 33 us -> 32.2 us  [call(): pl.pallas_call(kernel, out_shape=[jax.ShapeDtypeStruct(s, jnp.bfloat16) f...]
  transfers between devices with their start and end apart: 16 -> 16, of which waited for: 9 -> 9; matrix products, arithmetic and copies ran while one was open for 3% -> 3% of each run, Pallas kernels for 22% -> 21%
where the time goes in v2:
time: 73.6 us; the launch traced here: 73.4 us
  Pallas kernels  32.2 us (44%)
  starting transfers between devices  21 us (29%)
  waiting for transfers between devices  15.3 us (21%)
  local copies, waits for them, and re-layouts  4.51 us (6%)
    pallas_call x10, Pallas kernels, call(): pl.pallas_call(kernel, out_shape=[jax.ShapeDtypeStruct(s, jnp.bfloat16) f...  32.2 us
    ppermute x12, starting transfers between devices, over_time(): return lax.ppermute(array, 'tm', pairs)  17.4 us
    ppermute x4, waiting for transfers between devices, over_tiles(): return lax.ppermute(array, 'tile', pairs)  8.51 us
    ppermute x12, waiting for transfers between devices, over_time(): return lax.ppermute(array, 'tm', pairs)  6.75 us
    ppermute x4, starting transfers between devices, over_tiles(): return lax.ppermute(array, 'tile', pairs)  3.64 us
    unnamed x18, local copies, waits for them, and re-layouts  2.13 us
    reshape x1, local copies, waits for them, and re-layouts, on_device(): second_weight.reshape(27, C, C)  1.72 us
  transfers between devices with their start and end apart: 16, of which 9 were waited for; matrix products, arithmetic and copies ran while one was open for 3% of the time, Pallas kernels for 21%

profile of v2, /device:TPU:98, one launch (start us, length us, event | category | flops | bytes accessed | tf_op | source)
XLA Modules:
  0.0 73.4 jit_solution(4078977202941757302)
XLA Ops:
  0.0 0.0 copy-start
  0.0 1.4 %copy-done = bf16[1,1,96,7680]{3,2,1,0:T(8,128)(2,1)S(1)} copy-done((bf16[1,1,96,7680]{3,2,1,0:T(8,128)(2,1)S(1)}, bf16[1,1,96,7680]{3,2,1,0:T(8,128)(2,1)}, u32[]{:S(2)}) %copy-start) | copy-done | bytes 1474584
  1.4 0.0 copy-start.1
  1.4 1.3 %edges.1 = (bf16[96,320]{1,0:T(8,128)(2,1)S(1)}, bf16[96,320]{1,0:T(8,128)(2,1)S(1)}, bf16[96,256]{1,0:T(8,128)(2,1)S(1)}) custom-call(bf16[96,7680]{1,0:T(8,128)(2,1)S(1)} %bitcast.11), custom_call_target="tpu_custom_call" | custom-call | bytes 1474560 | tf_op jit(solution)/shard_map/edges/pallas_call | solution.py:41
  2.7 0.1 copy-done.1
  2.7 0.9 %cut.1 = (bf16[96,1920]{1,0:T(8,128)(2,1)S(1)}, bf16[96,1920]{1,0:T(8,128)(2,1)}, bf16[96,1920]{1,0:T(8,128)(2,1)}) custom-call(s32[1]{0:T(128)} %bitcast.me_ref, bf16[96,7680]{1,0:T(8,128)(2,1)S(1)} %bitcast.12), custom_call_target="tpu_custom_call" | custom-call | bytes 1105920 | tf_op jit(solution)/shard_map/cut/pallas_call | solution.py:41
  3.7 0.0 copy-start.8
  3.7 1.7 %collective-permute-start.4 = (bf16[96,1920]{1,0:T(8,128)(2,1)S(1)}, bf16[96,1920]{1,0:T(8,128)(2,1)S(1)}, u32[]{:S(2)}, u32[]{:S(2)}) collective-permute-start(bf16[96,1920]{1,0:T(8,128)(2,1)S(1)} %get-tuple-element.49), channel_id=1, source_target_pairs={{0,64},{64,128},{128,192},{192,0},{1,65},{65,129},{129,193},{193,1... | collective-permute-start | bytes 1105928 | tf_op jit(solution)/shard_map/ppermute | solution.py:381
  5.3 2.9 %collective-permute-start.5 = (bf16[96,1920]{1,0:T(8,128)(2,1)}, bf16[96,1920]{1,0:T(8,128)(2,1)S(1)}, u32[]{:S(2)}, u32[]{:S(2)}) collective-permute-start(bf16[96,1920]{1,0:T(8,128)(2,1)} %get-tuple-element.50), channel_id=1, source_target_pairs={{0,128},{64,192},{128,0},{192,64},{1,129},{65,193},{129,1},{193,65... | collective-permute-start | bytes 1105928 | tf_op jit(solution)/shard_map/ppermute | solution.py:381
  8.2 1.3 %collective-permute-start.6 = (bf16[96,1920]{1,0:T(8,128)(2,1)}, bf16[96,1920]{1,0:T(8,128)(2,1)}, u32[]{:S(2)}, u32[]{:S(2)}) collective-permute-start(bf16[96,1920]{1,0:T(8,128)(2,1)} %get-tuple-element.51), channel_id=1, source_target_pairs={{0,192},{64,0},{128,64},{192,128},{1,193},{65,1},{129,65},{193,129... | collective-permute-start | bytes 1105928 | tf_op jit(solution)/shard_map/ppermute | solution.py:381
  9.6 3.1 %collective-permute-start = (bf16[96,320]{1,0:T(8,128)(2,1)S(1)}, bf16[96,320]{1,0:T(8,128)(2,1)S(1)}, u32[]{:S(2)}, u32[]{:S(2)}) collective-permute-start(bf16[96,320]{1,0:T(8,128)(2,1)S(1)} %get-tuple-element.41), channel_id=1, source_target_pairs={{0,8},{1,9},{2,10},{3,11},{4,12},{5,13},{6,14},{7,15},{8,16},{9,17... | collective-permute-start | bytes 184328 | tf_op jit(solution)/shard_map/ppermute | solution.py:390
  12.7 0.0 collective-permute-start.1
  12.7 0.1 add_convert_fusion.exists
  12.8 1.9 %collective-permute-done.above = bf16[96,320]{1,0:T(8,128)(2,1)S(1)} collective-permute-done((bf16[96,320]{1,0:T(8,128)(2,1)S(1)}, bf16[96,320]{1,0:T(8,128)(2,1)S(1)}, u32[]{:S(2)}, u32[]{:S(2)}) %collective-permute-start) | collective-permute-done | bytes 61472 | tf_op jit(solution)/shard_map/ppermute | solution.py:390
  14.7 3.6 %collective-permute-done.1.below = bf16[96,320]{1,0:T(8,128)(2,1)S(1)} collective-permute-done((bf16[96,320]{1,0:T(8,128)(2,1)S(1)}, bf16[96,320]{1,0:T(8,128)(2,1)S(1)}, u32[]{:S(2)}, u32[]{:S(2)}) %collective-permute-start.1) | collective-permute-done | bytes 61472 | tf_op jit(solution)/shard_map/ppermute | solution.py:390
  18.3 0.9 %sides.1 = (bf16[96,256]{1,0:T(8,128)(2,1)S(1)}, bf16[4,96,640]{2,1,0:T(8,128)(2,1)S(1)}) custom-call(s32[1]{0:T(128)} %bitcast.me_ref, s32[4]{0:T(128)S(1)} %add_convert_fusion.exists, bf16[96,7680]{1,0:T(8,128)(2,1)S(1)} %bitcast.13, bf16[96,320]{1,0:T(8,128)(2,1)S(1)} %collective-permute-done.above, bf16[96,320]{1,0:T(8,128)(2,1)S(1)} %collective-permute-done.1.below, ...), custom_call_target="tpu_custom_call" | custom-call | bytes 196608 | tf_op jit(solution)/shard_map/sides/pallas_call | solution.py:41
  19.2 0.0 collective-permute-start.3
  19.2 0.5 collective-permute-start.2
  19.7 1.2 %collective-permute-done.3.from_right = bf16[96,256]{1,0:T(8,128)(2,1)S(1)} collective-permute-done((bf16[96,256]{1,0:T(8,128)(2,1)S(1)}, bf16[96,256]{1,0:T(8,128)(2,1)S(1)}, u32[]{:S(2)}, u32[]{:S(2)}) %collective-permute-start.3) | collective-permute-done | bytes 49184 | tf_op jit(solution)/shard_map/ppermute | solution.py:390
  20.9 1.8 %collective-permute-done.2.from_left = bf16[96,256]{1,0:T(8,128)(2,1)S(1)} collective-permute-done((bf16[96,256]{1,0:T(8,128)(2,1)S(1)}, bf16[96,256]{1,0:T(8,128)(2,1)S(1)}, u32[]{:S(2)}, u32[]{:S(2)}) %collective-permute-start.2) | collective-permute-done | bytes 49184 | tf_op jit(solution)/shard_map/ppermute | solution.py:390
  22.7 1.4 %rims.1 = (bf16[96,768]{1,0:T(8,128)(2,1)S(1)}, bf16[96,768]{1,0:T(8,128)(2,1)}, bf16[96,768]{1,0:T(8,128)(2,1)}, bf16[96,768]{1,0:T(8,128)(2,1)}) custom-call(s32[1]{0:T(128)} %bitcast.me_ref, s32[4]{0:T(128)S(1)} %add_convert_fusion.exists, bf16[4,96,640]{2,1,0:T(8,128)(2,1)S(1)} %get-tuple-element.44.rows, ...), custom_call_target="tpu_custom_call" | custom-call | bytes 589824 | tf_op jit(solution)/shard_map/rims/pallas_call | solution.py:41
  24.2 0.0 copy-start.3
  24.2 0.7 copy-done.3
  24.8 0.7 collective-permute-start.7
  25.5 0.8 %collective-permute-start.8 = (bf16[96,768]{1,0:T(8,128)(2,1)}, bf16[96,768]{1,0:T(8,128)(2,1)}, u32[]{:S(2)}, u32[]{:S(2)}) collective-permute-start(bf16[96,768]{1,0:T(8,128)(2,1)} %get-tuple-element.56), channel_id=1, source_target_pairs={{0,128},{64,192},{128,0},{192,64},{1,129},{65,193},{129,1},{193,65... | collective-permute-start | bytes 442376 | tf_op jit(solution)/shard_map/ppermute | solution.py:381
  26.3 0.0 collective-permute-done.4.m1
  26.3 1.9 %collective-permute-start.9 = (bf16[96,768]{1,0:T(8,128)(2,1)}, bf16[96,768]{1,0:T(8,128)(2,1)}, u32[]{:S(2)}, u32[]{:S(2)}) collective-permute-start(bf16[96,768]{1,0:T(8,128)(2,1)} %get-tuple-element.57), channel_id=1, source_target_pairs={{0,192},{64,0},{128,64},{192,128},{1,193},{65,1},{129,65},{193,129... | collective-permute-start | bytes 442376 | tf_op jit(solution)/shard_map/ppermute | solution.py:381
  28.2 0.0 copy-done.8
  28.2 0.7 reshape.17.first
  28.8 0.0 copy-start.2
  28.9 1.7 %reshape.18.second = bf16[27,96,96]{2,1,0:T(8,128)(2,1)S(1)} reshape(bf16[27,9216]{1,0:T(8,128)(2,1)} %param.12) | data formatting | bytes 995328 | tf_op jit(solution)/shard_map/reshape | solution.py:497
  30.6 0.5 weights.1
  31.1 0.0 copy-start.4
  31.1 0.0 copy-start.5
  31.1 0.0 copy-start.6
  31.1 0.0 copy-start.7
  31.1 0.0 collective-permute-done.5.m2
  31.2 0.0 collective-permute-done.6.m3
  31.2 0.0 copy-done.2
  31.2 3.4 %early.1 = (bf16[4,96,2688]{2,1,0:T(8,128)(2,1)S(1)}, bf16[4,96,2176]{2,1,0:T(8,128)(2,1)S(1)}) custom-call(s32[1]{0:T(128)} %bitcast.me_ref, f32[1,96]{1,0:T(1,128)S(1)} %bitcast.15, bf16[96,7680]{1,0:T(8,128)(2,1)S(1)} %bitcast.14, bf16[96,1920]{1,0:T(8,128)(2,1)S(1)} %collective-permute-done.4.m1, bf16[96,1920]{1,0:T(8,128)(2,1)S(1)} %collective-permute-done.5.m2, ...), custom_call_target="tpu_custom_call" | custom-call | bytes 8388608 | tf_op jit(solution)/shard_map/early/pallas_call | solution.py:41
  34.6 0.9 %collective-permute-done.7.refs_3_ = bf16[96,768]{1,0:T(8,128)(2,1)} collective-permute-done((bf16[96,768]{1,0:T(8,128)(2,1)}, bf16[96,768]{1,0:T(8,128)(2,1)}, u32[]{:S(2)}, u32[]{:S(2)}) %collective-permute-start.7) | collective-permute-done | bytes 147488 | tf_op jit(solution)/shard_map/ppermute | solution.py:381
  35.5 0.0 collective-permute-done.8.refs_4_
  35.5 0.6 collective-permute-done.9.refs_5_
  36.1 0.0 copy-done.4
  36.1 0.0 copy-done.5
  36.1 0.0 copy-done.6
  36.1 0.0 copy-done.7
  36.1 13.6 %block_0.1 = (bf16[96,1280]{1,0:T(8,128)(2,1)S(1)}, bf16[96,1280]{1,0:T(8,128)(2,1)S(1)}, bf16[96,1280]{1,0:T(8,128)(2,1)S(1)}, bf16[96,1280]{1,0:T(8,128)(2,1)S(1)}, bf16[4,96,384]{2,1,0:T(8,128)(2,1)S(1)}) custom-call(s32[1]{0:T(128)} %bitcast.me_ref, s32[4]{0:T(128)S(1)} %add_convert_fusion.exists, bf16[4,96,2176]{2,1,0:T(8,128)(2,1)S(1)} %get-tuple-element.52.refs_0_, ...), custom_call_target="tpu_custom_call" | custom-call | flops 4299816960 | bytes 8388608 | tf_op jit(solution)/shard_map/block_0/pallas_call | solution.py:41
  49.8 2.5 %collective-permute-start.13 = (bf16[96,1280]{1,0:T(8,128)(2,1)S(1)}, bf16[96,1280]{1,0:T(8,128)(2,1)S(1)}, u32[]{:S(2)}, u32[]{:S(2)}) collective-permute-start(bf16[96,1280]{1,0:T(8,128)(2,1)S(1)} %get-tuple-element.70), channel_id=1, source_target_pairs={{0,192},{64,0},{128,64},{192,128},{1,193},{65,1},{129,65},{193,129... | collective-permute-start | bytes 737288 | tf_op jit(solution)/shard_map/ppermute | solution.py:381
  52.3 0.0 collective-permute-start.14
  52.3 1.0 %collective-permute-start.15 = (bf16[96,1280]{1,0:T(8,128)(2,1)S(1)}, bf16[96,1280]{1,0:T(8,128)(2,1)S(1)}, u32[]{:S(2)}, u32[]{:S(2)}) collective-permute-start(bf16[96,1280]{1,0:T(8,128)(2,1)S(1)} %get-tuple-element.72), channel_id=1, source_target_pairs={{0,64},{64,128},{128,192},{192,0},{1,65},{65,129},{129,193},{193,1... | collective-permute-start | bytes 737288 | tf_op jit(solution)/shard_map/ppermute | solution.py:381
  53.2 8.3 %block_8.1 = (bf16[96,640]{1,0:T(8,128)(2,1)S(1)}, bf16[96,640]{1,0:T(8,128)(2,1)S(1)}, bf16[96,640]{1,0:T(8,128)(2,1)S(1)}, bf16[96,640]{1,0:T(8,128)(2,1)S(1)}) custom-call(s32[1]{0:T(128)} %bitcast.me_ref, s32[4]{0:T(128)S(1)} %add_convert_fusion.exists, bf16[4,96,2176]{2,1,0:T(8,128)(2,1)S(1)} %get-tuple-element.52.refs_0_, ...), custom_call_target="tpu_custom_call" | custom-call | flops 2388787200 | bytes 8388608 | tf_op jit(solution)/shard_map/block_8/pallas_call | solution.py:41
  61.5 2.4 %collective-permute-start.10 = (bf16[96,640]{1,0:T(8,128)(2,1)S(1)}, bf16[96,640]{1,0:T(8,128)(2,1)S(1)}, u32[]{:S(2)}, u32[]{:S(2)}) collective-permute-start(bf16[96,640]{1,0:T(8,128)(2,1)S(1)} %get-tuple-element.66), channel_id=1, source_target_pairs={{0,192},{64,0},{128,64},{192,128},{1,193},{65,1},{129,65},{193,129... | collective-permute-start | bytes 368648 | tf_op jit(solution)/shard_map/ppermute | solution.py:381
  63.9 2.3 %collective-permute-start.11 = (bf16[96,640]{1,0:T(8,128)(2,1)S(1)}, bf16[96,640]{1,0:T(8,128)(2,1)S(1)}, u32[]{:S(2)}, u32[]{:S(2)}) collective-permute-start(bf16[96,640]{1,0:T(8,128)(2,1)S(1)} %get-tuple-element.67), channel_id=1, source_target_pairs={{0,128},{64,192},{128,0},{192,64},{1,129},{65,193},{129,1},{193,65... | collective-permute-start | bytes 368648 | tf_op jit(solution)/shard_map/ppermute | solution.py:381
  66.2 0.0 collective-permute-done.13.refs_1_
  66.2 0.0 collective-permute-start.12
  66.2 0.0 collective-permute-done.14.refs_2_
  66.2 0.0 collective-permute-done.15.refs_3_
  66.2 1.0 %place_0.1.refs_4_ = bf16[96,7680]{1,0:T(8,128)(2,1)} custom-call(s32[1]{0:T(128)} %bitcast.me_ref, bf16[96,1280]{1,0:T(8,128)(2,1)S(1)} %get-tuple-element.69.refs_0_, bf16[96,1280]{1,0:T(8,128)(2,1)S(1)} %collective-permute-done.13.refs_1_, bf16[96,1280]{1,0:T(8,128)(2,1)S(1)} %collective-permute-done.14.refs_2_, ...), custom_call_target="tpu_custom_call" | custom-call | tf_op jit(solution)/shard_map/place_0/pallas_call | solution.py:41
  67.2 1.4 %collective-permute-done.10.refs_1_ = bf16[96,640]{1,0:T(8,128)(2,1)S(1)} collective-permute-done((bf16[96,640]{1,0:T(8,128)(2,1)S(1)}, bf16[96,640]{1,0:T(8,128)(2,1)S(1)}, u32[]{:S(2)}, u32[]{:S(2)}) %collective-permute-start.10) | collective-permute-done | bytes 122912 | tf_op jit(solution)/shard_map/ppermute | solution.py:381
  68.6 2.5 %collective-permute-done.11.refs_2_ = bf16[96,640]{1,0:T(8,128)(2,1)S(1)} collective-permute-done((bf16[96,640]{1,0:T(8,128)(2,1)S(1)}, bf16[96,640]{1,0:T(8,128)(2,1)S(1)}, u32[]{:S(2)}, u32[]{:S(2)}) %collective-permute-start.11) | collective-permute-done | bytes 122912 | tf_op jit(solution)/shard_map/ppermute | solution.py:381
  71.0 1.4 %collective-permute-done.12.refs_3_ = bf16[96,640]{1,0:T(8,128)(2,1)S(1)} collective-permute-done((bf16[96,640]{1,0:T(8,128)(2,1)S(1)}, bf16[96,640]{1,0:T(8,128)(2,1)S(1)}, u32[]{:S(2)}, u32[]{:S(2)}) %collective-permute-start.12) | collective-permute-done | bytes 122912 | tf_op jit(solution)/shard_map/ppermute | solution.py:381
  72.4 0.8 %place_8.1 = bf16[96,7680]{1,0:T(8,128)(2,1)} custom-call(s32[1]{0:T(128)} %bitcast.me_ref, bf16[96,640]{1,0:T(8,128)(2,1)S(1)} %get-tuple-element.65.refs_0_, bf16[96,640]{1,0:T(8,128)(2,1)S(1)} %collective-permute-done.10.refs_1_, bf16[96,640]{1,0:T(8,128)(2,1)S(1)} %collective-permute-done.11.refs_2_, ...), custom_call_target="tpu_custom_call", output_to_operand_aliasing={{}: (5, {})} | custom-call | tf_op jit(solution)/shard_map/place_8/pallas_call | solution.py:41
Async XLA Ops:
  0.0 1.4 %copy-start = (bf16[1,1,96,7680]{3,2,1,0:T(8,128)(2,1)S(1)}, bf16[1,1,96,7680]{3,2,1,0:T(8,128)(2,1)}, u32[]{:S(2)}) copy-start(bf16[1,1,96,7680]{3,2,1,0:T(8,128)(2,1)} %param.7) | copy-start | bytes 4423684
  1.4 1.4 %copy-start.1 = (bf16[1,1,96,7680]{3,2,1,0:T(8,128)(2,1)S(1)}, bf16[1,1,96,7680]{3,2,1,0:T(8,128)(2,1)}, u32[]{:S(2)}) copy-start(bf16[1,1,96,7680]{3,2,1,0:T(8,128)(2,1)} %param.7) | copy-start | bytes 4423684
  3.7 24.5 %copy-start.8 = (bf16[27,9216]{1,0:T(8,128)(2,1)S(1)}, bf16[27,9216]{1,0:T(8,128)(2,1)}, u32[]{:S(2)}) copy-start(bf16[27,9216]{1,0:T(8,128)(2,1)} %param.9) | copy-start | bytes 1492996
  3.7 22.6 %collective-permute-start.4 = (bf16[96,1920]{1,0:T(8,128)(2,1)S(1)}, bf16[96,1920]{1,0:T(8,128)(2,1)S(1)}, u32[]{:S(2)}, u32[]{:S(2)}) collective-permute-start(bf16[96,1920]{1,0:T(8,128)(2,1)S(1)} %get-tuple-element.49), channel_id=1, source_target_pairs={{0,64},{64,128},{128,192},{192,0},{1,65},{65,129},{129,193},{193,1... | collective-permute-start | bytes 1105928 | tf_op jit(solution)/shard_map/ppermute | solution.py:381
  5.3 25.8 %collective-permute-start.5 = (bf16[96,1920]{1,0:T(8,128)(2,1)}, bf16[96,1920]{1,0:T(8,128)(2,1)S(1)}, u32[]{:S(2)}, u32[]{:S(2)}) collective-permute-start(bf16[96,1920]{1,0:T(8,128)(2,1)} %get-tuple-element.50), channel_id=1, source_target_pairs={{0,128},{64,192},{128,0},{192,64},{1,129},{65,193},{129,1},{193,65... | collective-permute-start | bytes 1105928 | tf_op jit(solution)/shard_map/ppermute | solution.py:381
  8.2 22.9 %collective-permute-start.6 = (bf16[96,1920]{1,0:T(8,128)(2,1)}, bf16[96,1920]{1,0:T(8,128)(2,1)}, u32[]{:S(2)}, u32[]{:S(2)}) collective-permute-start(bf16[96,1920]{1,0:T(8,128)(2,1)} %get-tuple-element.51), channel_id=1, source_target_pairs={{0,192},{64,0},{128,64},{192,128},{1,193},{65,1},{129,65},{193,129... | collective-permute-start | bytes 1105928 | tf_op jit(solution)/shard_map/ppermute | solution.py:381
  9.6 5.1 %collective-permute-start = (bf16[96,320]{1,0:T(8,128)(2,1)S(1)}, bf16[96,320]{1,0:T(8,128)(2,1)S(1)}, u32[]{:S(2)}, u32[]{:S(2)}) collective-permute-start(bf16[96,320]{1,0:T(8,128)(2,1)S(1)} %get-tuple-element.41), channel_id=1, source_target_pairs={{0,8},{1,9},{2,10},{3,11},{4,12},{5,13},{6,14},{7,15},{8,16},{9,17... | collective-permute-start | bytes 184328 | tf_op jit(solution)/shard_map/ppermute | solution.py:390
  12.7 5.6 %collective-permute-start.1 = (bf16[96,320]{1,0:T(8,128)(2,1)S(1)}, bf16[96,320]{1,0:T(8,128)(2,1)S(1)}, u32[]{:S(2)}, u32[]{:S(2)}) collective-permute-start(bf16[96,320]{1,0:T(8,128)(2,1)S(1)} %get-tuple-element.42), channel_id=1, source_target_pairs={{0,56},{1,57},{2,58},{3,59},{4,60},{5,61},{6,62},{7,63},{8,0},{9,1... | collective-permute-start | bytes 184328 | tf_op jit(solution)/shard_map/ppermute | solution.py:390
  19.2 1.8 %collective-permute-start.3 = (bf16[96,256]{1,0:T(8,128)(2,1)S(1)}, bf16[96,256]{1,0:T(8,128)(2,1)S(1)}, u32[]{:S(2)}, u32[]{:S(2)}) collective-permute-start(bf16[96,256]{1,0:T(8,128)(2,1)S(1)} %get-tuple-element.45), channel_id=1, source_target_pairs={{0,7},{1,0},{2,1},{3,2},{4,3},{5,4},{6,5},{7,6},{8,15},{9,8},{10,9... | collective-permute-start | bytes 147464 | tf_op jit(solution)/shard_map/ppermute | solution.py:390
  19.2 3.5 %collective-permute-start.2 = (bf16[96,256]{1,0:T(8,128)(2,1)S(1)}, bf16[96,256]{1,0:T(8,128)(2,1)S(1)}, u32[]{:S(2)}, u32[]{:S(2)}) collective-permute-start(bf16[96,256]{1,0:T(8,128)(2,1)S(1)} %get-tuple-element.45), channel_id=1, source_target_pairs={{0,1},{1,2},{2,3},{3,4},{4,5},{5,6},{6,7},{7,0},{8,9},{9,10},{10,1... | collective-permute-start | bytes 147464 | tf_op jit(solution)/shard_map/ppermute | solution.py:390
  24.2 0.7 copy-start.3
  24.8 10.7 %collective-permute-start.7 = (bf16[96,768]{1,0:T(8,128)(2,1)}, bf16[96,768]{1,0:T(8,128)(2,1)}, u32[]{:S(2)}, u32[]{:S(2)}) collective-permute-start(bf16[96,768]{1,0:T(8,128)(2,1)} %get-tuple-element.55), channel_id=1, source_target_pairs={{0,64},{64,128},{128,192},{192,0},{1,65},{65,129},{129,193},{193,1... | collective-permute-start | bytes 442376 | tf_op jit(solution)/shard_map/ppermute | solution.py:381
  25.5 10.0 %collective-permute-start.8 = (bf16[96,768]{1,0:T(8,128)(2,1)}, bf16[96,768]{1,0:T(8,128)(2,1)}, u32[]{:S(2)}, u32[]{:S(2)}) collective-permute-start(bf16[96,768]{1,0:T(8,128)(2,1)} %get-tuple-element.56), channel_id=1, source_target_pairs={{0,128},{64,192},{128,0},{192,64},{1,129},{65,193},{129,1},{193,65... | collective-permute-start | bytes 442376 | tf_op jit(solution)/shard_map/ppermute | solution.py:381
  26.3 9.8 %collective-permute-start.9 = (bf16[96,768]{1,0:T(8,128)(2,1)}, bf16[96,768]{1,0:T(8,128)(2,1)}, u32[]{:S(2)}, u32[]{:S(2)}) collective-permute-start(bf16[96,768]{1,0:T(8,128)(2,1)} %get-tuple-element.57), channel_id=1, source_target_pairs={{0,192},{64,0},{128,64},{192,128},{1,193},{65,1},{129,65},{193,129... | collective-permute-start | bytes 442376 | tf_op jit(solution)/shard_map/ppermute | solution.py:381
  28.8 2.3 %copy-start.2 = (f32[96]{0:T(128)S(1)}, f32[96]{0:T(128)}, u32[]{:S(2)}) copy-start(f32[96]{0:T(128)} %param.8) | copy-start | bytes 1156
  31.1 5.0 %copy-start.4 = (bf16[96,768]{1,0:T(8,128)(2,1)S(1)}, bf16[96,768]{1,0:T(8,128)(2,1)}, u32[]{:S(2)}) copy-start(bf16[96,768]{1,0:T(8,128)(2,1)} %copy-done.3) | copy-start | bytes 442372
  31.1 5.0 %copy-start.5 = (f32[96]{0:T(128)S(1)}, f32[96]{0:T(128)}, u32[]{:S(2)}) copy-start(f32[96]{0:T(128)} %param.10) | copy-start | bytes 1156
  31.1 5.0 %copy-start.6 = (f32[96]{0:T(128)S(1)}, f32[96]{0:T(128)}, u32[]{:S(2)}) copy-start(f32[96]{0:T(128)} %param.11) | copy-start | bytes 1156
  31.1 5.0 %copy-start.7 = (f32[96]{0:T(128)S(1)}, f32[96]{0:T(128)}, u32[]{:S(2)}) copy-start(f32[96]{0:T(128)} %param.13) | copy-start | bytes 1156
  49.8 16.4 %collective-permute-start.13 = (bf16[96,1280]{1,0:T(8,128)(2,1)S(1)}, bf16[96,1280]{1,0:T(8,128)(2,1)S(1)}, u32[]{:S(2)}, u32[]{:S(2)}) collective-permute-start(bf16[96,1280]{1,0:T(8,128)(2,1)S(1)} %get-tuple-element.70), channel_id=1, source_target_pairs={{0,192},{64,0},{128,64},{192,128},{1,193},{65,1},{129,65},{193,129... | collective-permute-start | bytes 737288 | tf_op jit(solution)/shard_map/ppermute | solution.py:381
  52.3 14.0 %collective-permute-start.14 = (bf16[96,1280]{1,0:T(8,128)(2,1)S(1)}, bf16[96,1280]{1,0:T(8,128)(2,1)S(1)}, u32[]{:S(2)}, u32[]{:S(2)}) collective-permute-start(bf16[96,1280]{1,0:T(8,128)(2,1)S(1)} %get-tuple-element.71), channel_id=1, source_target_pairs={{0,128},{64,192},{128,0},{192,64},{1,129},{65,193},{129,1},{193,65... | collective-permute-start | bytes 737288 | tf_op jit(solution)/shard_map/ppermute | solution.py:381
  52.3 14.0 %collective-permute-start.15 = (bf16[96,1280]{1,0:T(8,128)(2,1)S(1)}, bf16[96,1280]{1,0:T(8,128)(2,1)S(1)}, u32[]{:S(2)}, u32[]{:S(2)}) collective-permute-start(bf16[96,1280]{1,0:T(8,128)(2,1)S(1)} %get-tuple-element.72), channel_id=1, source_target_pairs={{0,64},{64,128},{128,192},{192,0},{1,65},{65,129},{129,193},{193,1... | collective-permute-start | bytes 737288 | tf_op jit(solution)/shard_map/ppermute | solution.py:381
  61.5 7.0 %collective-permute-start.10 = (bf16[96,640]{1,0:T(8,128)(2,1)S(1)}, bf16[96,640]{1,0:T(8,128)(2,1)S(1)}, u32[]{:S(2)}, u32[]{:S(2)}) collective-permute-start(bf16[96,640]{1,0:T(8,128)(2,1)S(1)} %get-tuple-element.66), channel_id=1, source_target_pairs={{0,192},{64,0},{128,64},{192,128},{1,193},{65,1},{129,65},{193,129... | collective-permute-start | bytes 368648 | tf_op jit(solution)/shard_map/ppermute | solution.py:381
  63.9 7.1 %collective-permute-start.11 = (bf16[96,640]{1,0:T(8,128)(2,1)S(1)}, bf16[96,640]{1,0:T(8,128)(2,1)S(1)}, u32[]{:S(2)}, u32[]{:S(2)}) collective-permute-start(bf16[96,640]{1,0:T(8,128)(2,1)S(1)} %get-tuple-element.67), channel_id=1, source_target_pairs={{0,128},{64,192},{128,0},{192,64},{1,129},{65,193},{129,1},{193,65... | collective-permute-start | bytes 368648 | tf_op jit(solution)/shard_map/ppermute | solution.py:381
  66.2 6.2 %collective-permute-start.12 = (bf16[96,640]{1,0:T(8,128)(2,1)S(1)}, bf16[96,640]{1,0:T(8,128)(2,1)S(1)}, u32[]{:S(2)}, u32[]{:S(2)}) collective-permute-start(bf16[96,640]{1,0:T(8,128)(2,1)S(1)} %get-tuple-element.68), channel_id=1, source_target_pairs={{0,64},{64,128},{128,192},{192,0},{1,65},{65,129},{129,193},{193,1... | collective-permute-start | bytes 368648 | tf_op jit(solution)/shard_map/ppermute | solution.py:381

commit v3 on v2

--- a/solution.py
+++ b/solution.py
@@ -148,7 +148,7 @@
         outs[k][:, 4 * WT :] = mine[:, :128].astype(jnp.bfloat16)
 
 
-def early_kernel(me_ref, gain, x, m1, m2, m3, acts, placed, held, sems):
+def early_kernel(me_ref, gain, x, m1, m2, m3, acts, placed, held, flat, sems):
     me = me_ref[0]
     own = x.at[:, pl.ds(strip_at(0, me), LANES)]
     copies = [
@@ -161,8 +161,10 @@
     for t in range(FRAMES):
         for i in range(STRIP):
             placed[t, :, i * PITCH : i * PITCH + WT] = held[t, :, i * WT : (i + 1) * WT]
-        act = activated(placed[t, :, :2048].astype(jnp.float32), gain).astype(jnp.bfloat16)
-        acts[t, :, INSET : INSET + wide] = act[:, :wide]
+        for at in range(0, 2048, 128):
+            values = activated(placed[t, :, at : at + 128].astype(jnp.float32), gain)
+            flat[:, at : at + 128] = values.astype(jnp.bfloat16)
+        acts[t, :, INSET : INSET + wide] = flat[:, :wide]
 
 
 def up128(n):
@@ -501,7 +503,11 @@
     acts, placed = call(
         early_kernel,
         [(FRAMES, C, EXT), (FRAMES, C, PLACED)],
-        [pltpu.VMEM((FRAMES, C, LANES), jnp.bfloat16), dma((FRAMES,))],
+        [
+            pltpu.VMEM((FRAMES, C, LANES), jnp.bfloat16),
+            pltpu.VMEM((C, 2048), jnp.bfloat16),
+            dma((FRAMES,)),
+        ],
         smem(me_late) + vmem(first_gain[None]) + anywhere(x, *mains),
         mib=12,
         moved=8 * MIB,

time: 73.6 us -> 73.6 us (level)
  transfers between devices with their start and end apart: 16 -> 16, of which waited for: 9 -> 9; matrix products, arithmetic and copies ran while one was open for 3% -> 3% of each run, Pallas kernels for 21% -> 22%
where the time goes in v3:
time: 73.6 us; the launch traced here: 73.4 us
  Pallas kernels  32.5 us (44%)
  starting transfers between devices  21 us (29%)
  waiting for transfers between devices  15 us (20%)
  local copies, waits for them, and re-layouts  4.51 us (6%)
    pallas_call x10, Pallas kernels, call(): pl.pallas_call(kernel, out_shape=[jax.ShapeDtypeStruct(s, jnp.bfloat16) f...  32.5 us
    ppermute x12, starting transfers between devices, over_time(): return lax.ppermute(array, 'tm', pairs)  17.4 us
    ppermute x4, waiting for transfers between devices, over_tiles(): return lax.ppermute(array, 'tile', pairs)  8.51 us
    ppermute x12, waiting for transfers between devices, over_time(): return lax.ppermute(array, 'tm', pairs)  6.45 us
    ppermute x4, starting transfers between devices, over_tiles(): return lax.ppermute(array, 'tile', pairs)  3.64 us
    unnamed x18, local copies, waits for them, and re-layouts  2.13 us
    reshape x1, local copies, waits for them, and re-layouts, on_device(): second_weight.reshape(27, C, C)  1.72 us
  transfers between devices with their start and end apart: 16, of which 9 were waited for; matrix products, arithmetic and copies ran while one was open for 3% of the time, Pallas kernels for 22%

profile of v3, /device:TPU:98, one launch (start us, length us, event | category | flops | bytes accessed | tf_op | source)
XLA Modules:
  0.0 73.4 jit_solution(3279888162414272467)
XLA Ops:
  0.0 0.0 copy-start
  0.0 1.4 %copy-done = bf16[1,1,96,7680]{3,2,1,0:T(8,128)(2,1)S(1)} copy-done((bf16[1,1,96,7680]{3,2,1,0:T(8,128)(2,1)S(1)}, bf16[1,1,96,7680]{3,2,1,0:T(8,128)(2,1)}, u32[]{:S(2)}) %copy-start) | copy-done | bytes 1474584
  1.4 0.0 copy-start.1
  1.4 1.3 %edges.1 = (bf16[96,320]{1,0:T(8,128)(2,1)S(1)}, bf16[96,320]{1,0:T(8,128)(2,1)S(1)}, bf16[96,256]{1,0:T(8,128)(2,1)S(1)}) custom-call(bf16[96,7680]{1,0:T(8,128)(2,1)S(1)} %bitcast.11), custom_call_target="tpu_custom_call" | custom-call | bytes 1474560 | tf_op jit(solution)/shard_map/edges/pallas_call | solution.py:41
  2.7 0.1 copy-done.1
  2.7 0.9 %cut.1 = (bf16[96,1920]{1,0:T(8,128)(2,1)S(1)}, bf16[96,1920]{1,0:T(8,128)(2,1)}, bf16[96,1920]{1,0:T(8,128)(2,1)}) custom-call(s32[1]{0:T(128)} %bitcast.me_ref, bf16[96,7680]{1,0:T(8,128)(2,1)S(1)} %bitcast.12), custom_call_target="tpu_custom_call" | custom-call | bytes 1105920 | tf_op jit(solution)/shard_map/cut/pallas_call | solution.py:41
  3.7 0.0 copy-start.8
  3.7 1.7 %collective-permute-start.4 = (bf16[96,1920]{1,0:T(8,128)(2,1)S(1)}, bf16[96,1920]{1,0:T(8,128)(2,1)S(1)}, u32[]{:S(2)}, u32[]{:S(2)}) collective-permute-start(bf16[96,1920]{1,0:T(8,128)(2,1)S(1)} %get-tuple-element.49), channel_id=1, source_target_pairs={{0,64},{64,128},{128,192},{192,0},{1,65},{65,129},{129,193},{193,1... | collective-permute-start | bytes 1105928 | tf_op jit(solution)/shard_map/ppermute | solution.py:383
  5.3 2.9 %collective-permute-start.5 = (bf16[96,1920]{1,0:T(8,128)(2,1)}, bf16[96,1920]{1,0:T(8,128)(2,1)S(1)}, u32[]{:S(2)}, u32[]{:S(2)}) collective-permute-start(bf16[96,1920]{1,0:T(8,128)(2,1)} %get-tuple-element.50), channel_id=1, source_target_pairs={{0,128},{64,192},{128,0},{192,64},{1,129},{65,193},{129,1},{193,65... | collective-permute-start | bytes 1105928 | tf_op jit(solution)/shard_map/ppermute | solution.py:383
  8.2 1.3 %collective-permute-start.6 = (bf16[96,1920]{1,0:T(8,128)(2,1)}, bf16[96,1920]{1,0:T(8,128)(2,1)}, u32[]{:S(2)}, u32[]{:S(2)}) collective-permute-start(bf16[96,1920]{1,0:T(8,128)(2,1)} %get-tuple-element.51), channel_id=1, source_target_pairs={{0,192},{64,0},{128,64},{192,128},{1,193},{65,1},{129,65},{193,129... | collective-permute-start | bytes 1105928 | tf_op jit(solution)/shard_map/ppermute | solution.py:383
  9.6 3.1 %collective-permute-start = (bf16[96,320]{1,0:T(8,128)(2,1)S(1)}, bf16[96,320]{1,0:T(8,128)(2,1)S(1)}, u32[]{:S(2)}, u32[]{:S(2)}) collective-permute-start(bf16[96,320]{1,0:T(8,128)(2,1)S(1)} %get-tuple-element.41), channel_id=1, source_target_pairs={{0,8},{1,9},{2,10},{3,11},{4,12},{5,13},{6,14},{7,15},{8,16},{9,17... | collective-permute-start | bytes 184328 | tf_op jit(solution)/shard_map/ppermute | solution.py:392
  12.7 0.0 collective-permute-start.1
  12.7 0.1 add_convert_fusion.exists
  12.8 1.9 %collective-permute-done.above = bf16[96,320]{1,0:T(8,128)(2,1)S(1)} collective-permute-done((bf16[96,320]{1,0:T(8,128)(2,1)S(1)}, bf16[96,320]{1,0:T(8,128)(2,1)S(1)}, u32[]{:S(2)}, u32[]{:S(2)}) %collective-permute-start) | collective-permute-done | bytes 61472 | tf_op jit(solution)/shard_map/ppermute | solution.py:392
  14.7 3.6 %collective-permute-done.1.below = bf16[96,320]{1,0:T(8,128)(2,1)S(1)} collective-permute-done((bf16[96,320]{1,0:T(8,128)(2,1)S(1)}, bf16[96,320]{1,0:T(8,128)(2,1)S(1)}, u32[]{:S(2)}, u32[]{:S(2)}) %collective-permute-start.1) | collective-permute-done | bytes 61472 | tf_op jit(solution)/shard_map/ppermute | solution.py:392
  18.3 0.9 %sides.1 = (bf16[96,256]{1,0:T(8,128)(2,1)S(1)}, bf16[4,96,640]{2,1,0:T(8,128)(2,1)S(1)}) custom-call(s32[1]{0:T(128)} %bitcast.me_ref, s32[4]{0:T(128)S(1)} %add_convert_fusion.exists, bf16[96,7680]{1,0:T(8,128)(2,1)S(1)} %bitcast.13, bf16[96,320]{1,0:T(8,128)(2,1)S(1)} %collective-permute-done.above, bf16[96,320]{1,0:T(8,128)(2,1)S(1)} %collective-permute-done.1.below, ...), custom_call_target="tpu_custom_call" | custom-call | bytes 196608 | tf_op jit(solution)/shard_map/sides/pallas_call | solution.py:41
  19.2 0.0 collective-permute-start.3
  19.2 0.5 collective-permute-start.2
  19.7 1.2 %collective-permute-done.3.from_right = bf16[96,256]{1,0:T(8,128)(2,1)S(1)} collective-permute-done((bf16[96,256]{1,0:T(8,128)(2,1)S(1)}, bf16[96,256]{1,0:T(8,128)(2,1)S(1)}, u32[]{:S(2)}, u32[]{:S(2)}) %collective-permute-start.3) | collective-permute-done | bytes 49184 | tf_op jit(solution)/shard_map/ppermute | solution.py:392
  20.9 1.8 %collective-permute-done.2.from_left = bf16[96,256]{1,0:T(8,128)(2,1)S(1)} collective-permute-done((bf16[96,256]{1,0:T(8,128)(2,1)S(1)}, bf16[96,256]{1,0:T(8,128)(2,1)S(1)}, u32[]{:S(2)}, u32[]{:S(2)}) %collective-permute-start.2) | collective-permute-done | bytes 49184 | tf_op jit(solution)/shard_map/ppermute | solution.py:392
  22.7 1.4 %rims.1 = (bf16[96,768]{1,0:T(8,128)(2,1)S(1)}, bf16[96,768]{1,0:T(8,128)(2,1)}, bf16[96,768]{1,0:T(8,128)(2,1)}, bf16[96,768]{1,0:T(8,128)(2,1)}) custom-call(s32[1]{0:T(128)} %bitcast.me_ref, s32[4]{0:T(128)S(1)} %add_convert_fusion.exists, bf16[4,96,640]{2,1,0:T(8,128)(2,1)S(1)} %get-tuple-element.44.rows, ...), custom_call_target="tpu_custom_call" | custom-call | bytes 589824 | tf_op jit(solution)/shard_map/rims/pallas_call | solution.py:41
  24.2 0.0 copy-start.3
  24.2 0.7 copy-done.3
  24.8 0.7 collective-permute-start.7
  25.5 0.8 %collective-permute-start.8 = (bf16[96,768]{1,0:T(8,128)(2,1)}, bf16[96,768]{1,0:T(8,128)(2,1)}, u32[]{:S(2)}, u32[]{:S(2)}) collective-permute-start(bf16[96,768]{1,0:T(8,128)(2,1)} %get-tuple-element.56), channel_id=1, source_target_pairs={{0,128},{64,192},{128,0},{192,64},{1,129},{65,193},{129,1},{193,65... | collective-permute-start | bytes 442376 | tf_op jit(solution)/shard_map/ppermute | solution.py:383
  26.3 0.0 collective-permute-done.4.m1
  26.3 1.9 %collective-permute-start.9 = (bf16[96,768]{1,0:T(8,128)(2,1)}, bf16[96,768]{1,0:T(8,128)(2,1)}, u32[]{:S(2)}, u32[]{:S(2)}) collective-permute-start(bf16[96,768]{1,0:T(8,128)(2,1)} %get-tuple-element.57), channel_id=1, source_target_pairs={{0,192},{64,0},{128,64},{192,128},{1,193},{65,1},{129,65},{193,129... | collective-permute-start | bytes 442376 | tf_op jit(solution)/shard_map/ppermute | solution.py:383
  28.2 0.0 copy-done.8
  28.2 0.7 reshape.17.first
  28.8 0.0 copy-start.2
  28.9 1.7 %reshape.18.second = bf16[27,96,96]{2,1,0:T(8,128)(2,1)S(1)} reshape(bf16[27,9216]{1,0:T(8,128)(2,1)} %param.12) | data formatting | bytes 995328 | tf_op jit(solution)/shard_map/reshape | solution.py:499
  30.6 0.5 weights.1
  31.1 0.0 copy-start.4
  31.1 0.0 copy-start.5
  31.1 0.0 copy-start.6
  31.1 0.0 copy-start.7
  31.1 0.0 collective-permute-done.5.m2
  31.2 0.0 collective-permute-done.6.m3
  31.2 0.0 copy-done.2
  31.2 3.7 %early.1 = (bf16[4,96,2688]{2,1,0:T(8,128)(2,1)S(1)}, bf16[4,96,2176]{2,1,0:T(8,128)(2,1)S(1)}) custom-call(s32[1]{0:T(128)} %bitcast.me_ref, f32[1,96]{1,0:T(1,128)S(1)} %bitcast.15, bf16[96,7680]{1,0:T(8,128)(2,1)S(1)} %bitcast.14, bf16[96,1920]{1,0:T(8,128)(2,1)S(1)} %collective-permute-done.4.m1, bf16[96,1920]{1,0:T(8,128)(2,1)S(1)} %collective-permute-done.5.m2, ...), custom_call_target="tpu_custom_call" | custom-call | bytes 8388608 | tf_op jit(solution)/shard_map/early/pallas_call | solution.py:41
  34.9 0.6 collective-permute-done.7.refs_3_
  35.5 0.0 collective-permute-done.8.refs_4_
  35.5 0.6 collective-permute-done.9.refs_5_
  36.1 0.0 copy-done.4
  36.1 0.0 copy-done.5
  36.1 0.0 copy-done.6
  36.1 0.0 copy-done.7
  36.1 13.6 %block_0.1 = (bf16[96,1280]{1,0:T(8,128)(2,1)S(1)}, bf16[96,1280]{1,0:T(8,128)(2,1)S(1)}, bf16[96,1280]{1,0:T(8,128)(2,1)S(1)}, bf16[96,1280]{1,0:T(8,128)(2,1)S(1)}, bf16[4,96,384]{2,1,0:T(8,128)(2,1)S(1)}) custom-call(s32[1]{0:T(128)} %bitcast.me_ref, s32[4]{0:T(128)S(1)} %add_convert_fusion.exists, bf16[4,96,2176]{2,1,0:T(8,128)(2,1)S(1)} %get-tuple-element.52.refs_0_, ...), custom_call_target="tpu_custom_call" | custom-call | flops 4299816960 | bytes 8388608 | tf_op jit(solution)/shard_map/block_0/pallas_call | solution.py:41
  49.8 2.5 %collective-permute-start.13 = (bf16[96,1280]{1,0:T(8,128)(2,1)S(1)}, bf16[96,1280]{1,0:T(8,128)(2,1)S(1)}, u32[]{:S(2)}, u32[]{:S(2)}) collective-permute-start(bf16[96,1280]{1,0:T(8,128)(2,1)S(1)} %get-tuple-element.70), channel_id=1, source_target_pairs={{0,192},{64,0},{128,64},{192,128},{1,193},{65,1},{129,65},{193,129... | collective-permute-start | bytes 737288 | tf_op jit(solution)/shard_map/ppermute | solution.py:383
  52.3 0.0 collective-permute-start.14
  52.3 1.0 %collective-permute-start.15 = (bf16[96,1280]{1,0:T(8,128)(2,1)S(1)}, bf16[96,1280]{1,0:T(8,128)(2,1)S(1)}, u32[]{:S(2)}, u32[]{:S(2)}) collective-permute-start(bf16[96,1280]{1,0:T(8,128)(2,1)S(1)} %get-tuple-element.72), channel_id=1, source_target_pairs={{0,64},{64,128},{128,192},{192,0},{1,65},{65,129},{129,193},{193,1... | collective-permute-start | bytes 737288 | tf_op jit(solution)/shard_map/ppermute | solution.py:383
  53.2 8.3 %block_8.1 = (bf16[96,640]{1,0:T(8,128)(2,1)S(1)}, bf16[96,640]{1,0:T(8,128)(2,1)S(1)}, bf16[96,640]{1,0:T(8,128)(2,1)S(1)}, bf16[96,640]{1,0:T(8,128)(2,1)S(1)}) custom-call(s32[1]{0:T(128)} %bitcast.me_ref, s32[4]{0:T(128)S(1)} %add_convert_fusion.exists, bf16[4,96,2176]{2,1,0:T(8,128)(2,1)S(1)} %get-tuple-element.52.refs_0_, ...), custom_call_target="tpu_custom_call" | custom-call | flops 2388787200 | bytes 8388608 | tf_op jit(solution)/shard_map/block_8/pallas_call | solution.py:41
  61.5 2.4 %collective-permute-start.10 = (bf16[96,640]{1,0:T(8,128)(2,1)S(1)}, bf16[96,640]{1,0:T(8,128)(2,1)S(1)}, u32[]{:S(2)}, u32[]{:S(2)}) collective-permute-start(bf16[96,640]{1,0:T(8,128)(2,1)S(1)} %get-tuple-element.66), channel_id=1, source_target_pairs={{0,192},{64,0},{128,64},{192,128},{1,193},{65,1},{129,65},{193,129... | collective-permute-start | bytes 368648 | tf_op jit(solution)/shard_map/ppermute | solution.py:383
  63.9 2.3 %collective-permute-start.11 = (bf16[96,640]{1,0:T(8,128)(2,1)S(1)}, bf16[96,640]{1,0:T(8,128)(2,1)S(1)}, u32[]{:S(2)}, u32[]{:S(2)}) collective-permute-start(bf16[96,640]{1,0:T(8,128)(2,1)S(1)} %get-tuple-element.67), channel_id=1, source_target_pairs={{0,128},{64,192},{128,0},{192,64},{1,129},{65,193},{129,1},{193,65... | collective-permute-start | bytes 368648 | tf_op jit(solution)/shard_map/ppermute | solution.py:383
  66.2 0.0 collective-permute-done.13.refs_1_
  66.2 0.0 collective-permute-start.12
  66.2 0.0 collective-permute-done.14.refs_2_
  66.2 0.0 collective-permute-done.15.refs_3_
  66.2 1.0 %place_0.1.refs_4_ = bf16[96,7680]{1,0:T(8,128)(2,1)} custom-call(s32[1]{0:T(128)} %bitcast.me_ref, bf16[96,1280]{1,0:T(8,128)(2,1)S(1)} %get-tuple-element.69.refs_0_, bf16[96,1280]{1,0:T(8,128)(2,1)S(1)} %collective-permute-done.13.refs_1_, bf16[96,1280]{1,0:T(8,128)(2,1)S(1)} %collective-permute-done.14.refs_2_, ...), custom_call_target="tpu_custom_call" | custom-call | tf_op jit(solution)/shard_map/place_0/pallas_call | solution.py:41
  67.2 1.4 %collective-permute-done.10.refs_1_ = bf16[96,640]{1,0:T(8,128)(2,1)S(1)} collective-permute-done((bf16[96,640]{1,0:T(8,128)(2,1)S(1)}, bf16[96,640]{1,0:T(8,128)(2,1)S(1)}, u32[]{:S(2)}, u32[]{:S(2)}) %collective-permute-start.10) | collective-permute-done | bytes 122912 | tf_op jit(solution)/shard_map/ppermute | solution.py:383
  68.6 2.5 %collective-permute-done.11.refs_2_ = bf16[96,640]{1,0:T(8,128)(2,1)S(1)} collective-permute-done((bf16[96,640]{1,0:T(8,128)(2,1)S(1)}, bf16[96,640]{1,0:T(8,128)(2,1)S(1)}, u32[]{:S(2)}, u32[]{:S(2)}) %collective-permute-start.11) | collective-permute-done | bytes 122912 | tf_op jit(solution)/shard_map/ppermute | solution.py:383
  71.0 1.4 %collective-permute-done.12.refs_3_ = bf16[96,640]{1,0:T(8,128)(2,1)S(1)} collective-permute-done((bf16[96,640]{1,0:T(8,128)(2,1)S(1)}, bf16[96,640]{1,0:T(8,128)(2,1)S(1)}, u32[]{:S(2)}, u32[]{:S(2)}) %collective-permute-start.12) | collective-permute-done | bytes 122912 | tf_op jit(solution)/shard_map/ppermute | solution.py:383
  72.4 0.8 %place_8.1 = bf16[96,7680]{1,0:T(8,128)(2,1)} custom-call(s32[1]{0:T(128)} %bitcast.me_ref, bf16[96,640]{1,0:T(8,128)(2,1)S(1)} %get-tuple-element.65.refs_0_, bf16[96,640]{1,0:T(8,128)(2,1)S(1)} %collective-permute-done.10.refs_1_, bf16[96,640]{1,0:T(8,128)(2,1)S(1)} %collective-permute-done.11.refs_2_, ...), custom_call_target="tpu_custom_call", output_to_operand_aliasing={{}: (5, {})} | custom-call | tf_op jit(solution)/shard_map/place_8/pallas_call | solution.py:41
Async XLA Ops:
  0.0 1.4 %copy-start = (bf16[1,1,96,7680]{3,2,1,0:T(8,128)(2,1)S(1)}, bf16[1,1,96,7680]{3,2,1,0:T(8,128)(2,1)}, u32[]{:S(2)}) copy-start(bf16[1,1,96,7680]{3,2,1,0:T(8,128)(2,1)} %param.7) | copy-start | bytes 4423684
  1.4 1.4 %copy-start.1 = (bf16[1,1,96,7680]{3,2,1,0:T(8,128)(2,1)S(1)}, bf16[1,1,96,7680]{3,2,1,0:T(8,128)(2,1)}, u32[]{:S(2)}) copy-start(bf16[1,1,96,7680]{3,2,1,0:T(8,128)(2,1)} %param.7) | copy-start | bytes 4423684
  3.7 24.5 %copy-start.8 = (bf16[27,9216]{1,0:T(8,128)(2,1)S(1)}, bf16[27,9216]{1,0:T(8,128)(2,1)}, u32[]{:S(2)}) copy-start(bf16[27,9216]{1,0:T(8,128)(2,1)} %param.9) | copy-start | bytes 1492996
  3.7 22.6 %collective-permute-start.4 = (bf16[96,1920]{1,0:T(8,128)(2,1)S(1)}, bf16[96,1920]{1,0:T(8,128)(2,1)S(1)}, u32[]{:S(2)}, u32[]{:S(2)}) collective-permute-start(bf16[96,1920]{1,0:T(8,128)(2,1)S(1)} %get-tuple-element.49), channel_id=1, source_target_pairs={{0,64},{64,128},{128,192},{192,0},{1,65},{65,129},{129,193},{193,1... | collective-permute-start | bytes 1105928 | tf_op jit(solution)/shard_map/ppermute | solution.py:383
  5.3 25.8 %collective-permute-start.5 = (bf16[96,1920]{1,0:T(8,128)(2,1)}, bf16[96,1920]{1,0:T(8,128)(2,1)S(1)}, u32[]{:S(2)}, u32[]{:S(2)}) collective-permute-start(bf16[96,1920]{1,0:T(8,128)(2,1)} %get-tuple-element.50), channel_id=1, source_target_pairs={{0,128},{64,192},{128,0},{192,64},{1,129},{65,193},{129,1},{193,65... | collective-permute-start | bytes 1105928 | tf_op jit(solution)/shard_map/ppermute | solution.py:383
  8.2 22.9 %collective-permute-start.6 = (bf16[96,1920]{1,0:T(8,128)(2,1)}, bf16[96,1920]{1,0:T(8,128)(2,1)}, u32[]{:S(2)}, u32[]{:S(2)}) collective-permute-start(bf16[96,1920]{1,0:T(8,128)(2,1)} %get-tuple-element.51), channel_id=1, source_target_pairs={{0,192},{64,0},{128,64},{192,128},{1,193},{65,1},{129,65},{193,129... | collective-permute-start | bytes 1105928 | tf_op jit(solution)/shard_map/ppermute | solution.py:383
  9.6 5.1 %collective-permute-start = (bf16[96,320]{1,0:T(8,128)(2,1)S(1)}, bf16[96,320]{1,0:T(8,128)(2,1)S(1)}, u32[]{:S(2)}, u32[]{:S(2)}) collective-permute-start(bf16[96,320]{1,0:T(8,128)(2,1)S(1)} %get-tuple-element.41), channel_id=1, source_target_pairs={{0,8},{1,9},{2,10},{3,11},{4,12},{5,13},{6,14},{7,15},{8,16},{9,17... | collective-permute-start | bytes 184328 | tf_op jit(solution)/shard_map/ppermute | solution.py:392
  12.7 5.6 %collective-permute-start.1 = (bf16[96,320]{1,0:T(8,128)(2,1)S(1)}, bf16[96,320]{1,0:T(8,128)(2,1)S(1)}, u32[]{:S(2)}, u32[]{:S(2)}) collective-permute-start(bf16[96,320]{1,0:T(8,128)(2,1)S(1)} %get-tuple-element.42), channel_id=1, source_target_pairs={{0,56},{1,57},{2,58},{3,59},{4,60},{5,61},{6,62},{7,63},{8,0},{9,1... | collective-permute-start | bytes 184328 | tf_op jit(solution)/shard_map/ppermute | solution.py:392
  19.2 1.8 %collective-permute-start.3 = (bf16[96,256]{1,0:T(8,128)(2,1)S(1)}, bf16[96,256]{1,0:T(8,128)(2,1)S(1)}, u32[]{:S(2)}, u32[]{:S(2)}) collective-permute-start(bf16[96,256]{1,0:T(8,128)(2,1)S(1)} %get-tuple-element.45), channel_id=1, source_target_pairs={{0,7},{1,0},{2,1},{3,2},{4,3},{5,4},{6,5},{7,6},{8,15},{9,8},{10,9... | collective-permute-start | bytes 147464 | tf_op jit(solution)/shard_map/ppermute | solution.py:392
  19.2 3.5 %collective-permute-start.2 = (bf16[96,256]{1,0:T(8,128)(2,1)S(1)}, bf16[96,256]{1,0:T(8,128)(2,1)S(1)}, u32[]{:S(2)}, u32[]{:S(2)}) collective-permute-start(bf16[96,256]{1,0:T(8,128)(2,1)S(1)} %get-tuple-element.45), channel_id=1, source_target_pairs={{0,1},{1,2},{2,3},{3,4},{4,5},{5,6},{6,7},{7,0},{8,9},{9,10},{10,1... | collective-permute-start | bytes 147464 | tf_op jit(solution)/shard_map/ppermute | solution.py:392
  24.2 0.7 copy-start.3
  24.8 10.7 %collective-permute-start.7 = (bf16[96,768]{1,0:T(8,128)(2,1)}, bf16[96,768]{1,0:T(8,128)(2,1)}, u32[]{:S(2)}, u32[]{:S(2)}) collective-permute-start(bf16[96,768]{1,0:T(8,128)(2,1)} %get-tuple-element.55), channel_id=1, source_target_pairs={{0,64},{64,128},{128,192},{192,0},{1,65},{65,129},{129,193},{193,1... | collective-permute-start | bytes 442376 | tf_op jit(solution)/shard_map/ppermute | solution.py:383
  25.5 10.0 %collective-permute-start.8 = (bf16[96,768]{1,0:T(8,128)(2,1)}, bf16[96,768]{1,0:T(8,128)(2,1)}, u32[]{:S(2)}, u32[]{:S(2)}) collective-permute-start(bf16[96,768]{1,0:T(8,128)(2,1)} %get-tuple-element.56), channel_id=1, source_target_pairs={{0,128},{64,192},{128,0},{192,64},{1,129},{65,193},{129,1},{193,65... | collective-permute-start | bytes 442376 | tf_op jit(solution)/shard_map/ppermute | solution.py:383
  26.3 9.8 %collective-permute-start.9 = (bf16[96,768]{1,0:T(8,128)(2,1)}, bf16[96,768]{1,0:T(8,128)(2,1)}, u32[]{:S(2)}, u32[]{:S(2)}) collective-permute-start(bf16[96,768]{1,0:T(8,128)(2,1)} %get-tuple-element.57), channel_id=1, source_target_pairs={{0,192},{64,0},{128,64},{192,128},{1,193},{65,1},{129,65},{193,129... | collective-permute-start | bytes 442376 | tf_op jit(solution)/shard_map/ppermute | solution.py:383
  28.8 2.3 %copy-start.2 = (f32[96]{0:T(128)S(1)}, f32[96]{0:T(128)}, u32[]{:S(2)}) copy-start(f32[96]{0:T(128)} %param.8) | copy-start | bytes 1156
  31.1 5.0 %copy-start.4 = (bf16[96,768]{1,0:T(8,128)(2,1)S(1)}, bf16[96,768]{1,0:T(8,128)(2,1)}, u32[]{:S(2)}) copy-start(bf16[96,768]{1,0:T(8,128)(2,1)} %copy-done.3) | copy-start | bytes 442372
  31.1 5.0 %copy-start.5 = (f32[96]{0:T(128)S(1)}, f32[96]{0:T(128)}, u32[]{:S(2)}) copy-start(f32[96]{0:T(128)} %param.10) | copy-start | bytes 1156
  31.1 5.0 %copy-start.6 = (f32[96]{0:T(128)S(1)}, f32[96]{0:T(128)}, u32[]{:S(2)}) copy-start(f32[96]{0:T(128)} %param.11) | copy-start | bytes 1156
  31.1 5.0 %copy-start.7 = (f32[96]{0:T(128)S(1)}, f32[96]{0:T(128)}, u32[]{:S(2)}) copy-start(f32[96]{0:T(128)} %param.13) | copy-start | bytes 1156
  49.8 16.4 %collective-permute-start.13 = (bf16[96,1280]{1,0:T(8,128)(2,1)S(1)}, bf16[96,1280]{1,0:T(8,128)(2,1)S(1)}, u32[]{:S(2)}, u32[]{:S(2)}) collective-permute-start(bf16[96,1280]{1,0:T(8,128)(2,1)S(1)} %get-tuple-element.70), channel_id=1, source_target_pairs={{0,192},{64,0},{128,64},{192,128},{1,193},{65,1},{129,65},{193,129... | collective-permute-start | bytes 737288 | tf_op jit(solution)/shard_map/ppermute | solution.py:383
  52.3 14.0 %collective-permute-start.14 = (bf16[96,1280]{1,0:T(8,128)(2,1)S(1)}, bf16[96,1280]{1,0:T(8,128)(2,1)S(1)}, u32[]{:S(2)}, u32[]{:S(2)}) collective-permute-start(bf16[96,1280]{1,0:T(8,128)(2,1)S(1)} %get-tuple-element.71), channel_id=1, source_target_pairs={{0,128},{64,192},{128,0},{192,64},{1,129},{65,193},{129,1},{193,65... | collective-permute-start | bytes 737288 | tf_op jit(solution)/shard_map/ppermute | solution.py:383
  52.3 14.0 %collective-permute-start.15 = (bf16[96,1280]{1,0:T(8,128)(2,1)S(1)}, bf16[96,1280]{1,0:T(8,128)(2,1)S(1)}, u32[]{:S(2)}, u32[]{:S(2)}) collective-permute-start(bf16[96,1280]{1,0:T(8,128)(2,1)S(1)} %get-tuple-element.72), channel_id=1, source_target_pairs={{0,64},{64,128},{128,192},{192,0},{1,65},{65,129},{129,193},{193,1... | collective-permute-start | bytes 737288 | tf_op jit(solution)/shard_map/ppermute | solution.py:383
  61.5 7.0 %collective-permute-start.10 = (bf16[96,640]{1,0:T(8,128)(2,1)S(1)}, bf16[96,640]{1,0:T(8,128)(2,1)S(1)}, u32[]{:S(2)}, u32[]{:S(2)}) collective-permute-start(bf16[96,640]{1,0:T(8,128)(2,1)S(1)} %get-tuple-element.66), channel_id=1, source_target_pairs={{0,192},{64,0},{128,64},{192,128},{1,193},{65,1},{129,65},{193,129... | collective-permute-start | bytes 368648 | tf_op jit(solution)/shard_map/ppermute | solution.py:383
  63.9 7.1 %collective-permute-start.11 = (bf16[96,640]{1,0:T(8,128)(2,1)S(1)}, bf16[96,640]{1,0:T(8,128)(2,1)S(1)}, u32[]{:S(2)}, u32[]{:S(2)}) collective-permute-start(bf16[96,640]{1,0:T(8,128)(2,1)S(1)} %get-tuple-element.67), channel_id=1, source_target_pairs={{0,128},{64,192},{128,0},{192,64},{1,129},{65,193},{129,1},{193,65... | collective-permute-start | bytes 368648 | tf_op jit(solution)/shard_map/ppermute | solution.py:383
  66.2 6.2 %collective-permute-start.12 = (bf16[96,640]{1,0:T(8,128)(2,1)S(1)}, bf16[96,640]{1,0:T(8,128)(2,1)S(1)}, u32[]{:S(2)}, u32[]{:S(2)}) collective-permute-start(bf16[96,640]{1,0:T(8,128)(2,1)S(1)} %get-tuple-element.68), channel_id=1, source_target_pairs={{0,64},{64,128},{128,192},{192,0},{1,65},{65,129},{129,193},{193,1... | collective-permute-start | bytes 368648 | tf_op jit(solution)/shard_map/ppermute | solution.py:383
